TPU v7x, 512 devices: a whole 4x8x8 slice. The times are simulated.
512 devices in a mesh: views: 8 (over y), tiles: 64 (over x, z, core).
Axes of the slice: x: 4, y: 8, z: 8, core: 2. Of those that a mesh axis runs over, the one named last changes fastest.
Arguments:
- linear_point: float32 [59, 32768], P(None, 'tiles'), may hold values from -6 to 6
- right_side: float32 [59, 32768], P(None, 'tiles'), may hold values from -75 to 75
- damping: float32 [59, 32768], P(None, 'tiles'), may hold values from 0.2 to 2
- projection: float32 [8, 59, 16], P('views'), may hold values from -0.75 to 0.75
- pixel_basis: float32 [8, 64, 12, 128], P('views', 'tiles'), may hold values from -1.8 to 1.8
- pixel_weight: float32 [8, 64, 128], P('views', 'tiles'), may hold values from 50 to 500
- depth_order: int32 [8, 64, 512], P('views', 'tiles'), may hold values from 0 to 511, each once within a row
- tile_dest: int32 [8, 4096, 1], P('views', 'tiles'), may hold values from 0 to 63; in each aligned block of 64 rows (0 to 63, 64 to 127, ..., all dimensions but the last counted through in order) at most 2 rows name the same one
- block_depth: int32 [8, 4096], P('views', 'tiles'), may hold values from 0 to 4095, each once within a row
Outputs:
- solution: float32 [59, 32768], P(None, 'tiles')
- residual: float32 [59, 32768], P(None, 'tiles')
Inputs may be any that keep to these rules, and one draw needn't show every extreme that they name: `tile_dest`: each block of one owner in one view names one tile; no tile is named by more than 2 blocks of one owner in one view, a bound that the blocks of some owner reach; every tile is named by some block of every view. `depth_order`: for each view and owner, a permutation of the owner's local Gaussian numbers. `block_depth`: for each view, a permutation of the block numbers.
All inputs are finite; a program needn't handle non-finite values.
Results may differ from a plain program's by a relative error of at most 0.007.
Values sent between devices are 32-bit elements; how exact they have to be, the bound alone decides.
No kernel may reach another device: no remote copies, remote signals or barrier semaphores. Data moves between devices by JAX's collectives and lax.ppermute only.
A program may use at most 64 MiB of HBM per device.

v0:
```python
import jax
import jax.numpy as jnp
from jax import lax
from jax.sharding import PartitionSpec as P

ITERS = 2


PRECISE = lax.Precision.HIGHEST
OFFSET = 6.0


def blend(blocks, depth_marks, tile_basis):
    logits = (
        blocks[:, 0, :, None]
        - OFFSET
        + jnp.einsum("skr,kp->srp", blocks[:, 4:, :], tile_basis, precision=PRECISE)
    )
    alphas = jax.nn.sigmoid(logits)
    log_clear = -jax.nn.softplus(logits)
    before = jnp.cumsum(log_clear, axis=1) - log_clear
    colors = jnp.einsum(
        "scr,srp->scp", blocks[:, 1:4, :], alphas * jnp.exp(before), precision=PRECISE
    )
    filled = (depth_marks > 0.0).astype(jnp.float32)
    colors = colors * filled[:, None, None]
    through = jnp.sum(log_clear, axis=1) * filled[:, None]
    earlier = ((depth_marks[None, :] < depth_marks[:, None]) & (depth_marks[None, :] > 0.0)).astype(
        jnp.float32
    )
    ahead = jnp.dot(earlier, through, precision=PRECISE)
    return jnp.einsum("sp,scp->cp", jnp.exp(ahead), colors, precision=PRECISE)


def body(
    linear_point,
    right_side,
    damping,
    projection,
    pixel_basis,
    pixel_weight,
    depth_order,
    tile_dest,
    block_depth,
):
    view_proj = projection[0]
    tile_basis = pixel_basis[0, 0]
    tile_weight = pixel_weight[0, 0]
    local_order = depth_order[0, 0]
    local_dest = tile_dest[0, :, 0]
    local_depth = block_depth[0]
    owners = lax.axis_size("tiles")
    count = local_dest.shape[0]
    gauss_local = local_order.shape[0]
    per_block = gauss_local // count
    capacity = max(2, count // owners)
    slots = owners * capacity
    shared = local_dest[None, :] == local_dest[:, None]
    before = jnp.arange(count)[None, :] < jnp.arange(count)[:, None]
    position = jnp.sum((shared & before).astype(jnp.int32), axis=1)
    slot_of = local_dest * capacity + position
    block_of = jnp.zeros((slots,), jnp.int32).at[slot_of].set(jnp.arange(count, dtype=jnp.int32))
    occupied = jnp.zeros((slots,), jnp.float32).at[slot_of].set(1.0)
    marks_send = (
        jnp.zeros((slots,), jnp.float32).at[slot_of].set(local_depth.astype(jnp.float32) + 1.0)
    )
    inverse = (
        jnp.zeros((gauss_local,), jnp.int32)
        .at[local_order]
        .set(jnp.arange(gauss_local, dtype=jnp.int32))
    )

    def to_slots(vector):
        picked = jnp.take(vector, local_order, axis=1).reshape(vector.shape[0], count, per_block)
        blocks = jnp.einsum("kf,kbr->bfr", view_proj, picked, precision=PRECISE)
        return jnp.take(blocks, block_of, axis=0) * occupied[:, None, None]

    def from_slots(returned):
        blocks = jnp.take(returned, slot_of, axis=0)
        params_sorted = jnp.einsum("kf,bfr->kbr", view_proj, blocks, precision=PRECISE)
        return jnp.take(params_sorted.reshape(view_proj.shape[0], gauss_local), inverse, axis=1)

    primal_send = to_slots(linear_point)

    def apply_normal(vector):
        primal_now, tangent_recv, marks_now = (
            lax.all_to_all(primal_send, "tiles", split_axis=0, concat_axis=0, tiled=True),
            lax.all_to_all(to_slots(vector), "tiles", split_axis=0, concat_axis=0, tiled=True),
            lax.all_to_all(marks_send, "tiles", split_axis=0, concat_axis=0, tiled=True),
        )

        def blend_now(blocks):
            return blend(blocks, marks_now, tile_basis)

        image_tangent = jax.jvp(blend_now, (primal_now,), (tangent_recv,))[1]
        unused_out, pull = jax.vjp(blend_now, primal_now)
        cotangent = pull(image_tangent * tile_weight[None, :])[0]
        returned = lax.all_to_all(cotangent, "tiles", split_axis=0, concat_axis=0, tiled=True)
        return from_slots(returned)

    def squares(vector):
        return lax.psum(jnp.sum(vector * vector), "tiles")

    solution = jnp.zeros_like(right_side)
    residual = right_side
    direction = right_side
    norm_now = squares(residual)
    for iteration in range(ITERS):
        product = lax.psum(apply_normal(direction), "views") + damping * direction
        step_size = norm_now / lax.psum(jnp.sum(direction * product), "tiles")
        solution = solution + step_size * direction
        residual = residual - step_size * product
        norm_next = squares(residual)
        direction = residual + norm_next / norm_now * direction
        norm_now = norm_next
    return (solution, residual)


def solution(mesh):
    in_specs = (
        P(None, "tiles"),
        P(None, "tiles"),
        P(None, "tiles"),
        P("views", None, None),
        P("views", "tiles", None, None),
        P("views", "tiles", None),
        P("views", "tiles", None),
        P("views", "tiles", None),
        P("views", "tiles"),
    )
    out_specs = (P(None, "tiles"), P(None, "tiles"))
    return jax.shard_map(body, mesh=mesh, in_specs=in_specs, out_specs=out_specs, check_vma=False)
```

profile of v0, /device:TPU:1, one launch (start us, length us, event | category | flops | bytes accessed | tf_op | source)
XLA Modules:
  0.0 712.2 jit_solution(17336740593216540511)
XLA Ops:
  8.7 0.8 scatter_custom_fusion.2
  10.2 14.8 %all-to-all-start.2 = ((f32[64,2,1]{1,2,0:T(1,128)}), f32[64,2,1]{1,2,0:T(1,128)S(1)}, u32[]{:S(2)}, u32[]{:S(2)}) async-start(f32[64,2,1]{1,2,0:T(1,128)} %bitcast.28), calls=%async_computation.2 | async-start | bytes 65536 | tf_op jit(solution)/shard_map/all_to_all | solution.py:89
  26.4 0.8 scatter_custom_fusion
  27.9 2.4 scatter_custom_fusion.3
  30.6 0.8 copy-done.11
  31.5 1.0 gather_fusion
  32.5 1.0 gather_fusion.2
  35.5 0.8 gather_fusion.1
  36.3 0.8 gather_fusion.3
  37.1 0.8 scatter_custom_fusion.1
  38.4 0.9 reshape.319
  39.3 0.9 reshape.321
  40.1 10.3 %all-to-all-start.1 = ((f32[64,1,256]{2,1,0:T(1,128)}), f32[64,1,256]{2,1,0:T(1,128)S(1)}, u32[]{:S(2)}, u32[]{:S(2)}) async-start(f32[64,1,256]{2,1,0:T(1,128)} %reshape.319), calls=%async_computation.1 | async-start | bytes 131072 | tf_op jit(solution)/shard_map/all_to_all | solution.py:87
  51.0 0.8 reduce.17
  52.0 8.3 %all-to-all-done.1 = f32[64,1,256]{2,1,0:T(1,128)S(1)} async-done(((f32[64,1,256]{2,1,0:T(1,128)}), f32[64,1,256]{2,1,0:T(1,128)S(1)}, u32[]{:S(2)}, u32[]{:S(2)}) %all-to-all-start.1) | async-done | bytes 65568 | tf_op jit(solution)/shard_map/all_to_all | solution.py:87
  60.2 4.9 all-to-all-start
  65.7 0.8 reduce.18
  67.1 7.5 %all-to-all-done = f32[64,1,256]{2,1,0:T(1,128)S(1)} async-done(((f32[64,1,256]{2,1,0:T(1,128)}), f32[64,1,256]{2,1,0:T(1,128)S(1)}, u32[]{:S(2)}, u32[]{:S(2)}) %all-to-all-start) | async-done | bytes 65568 | tf_op jit(solution)/shard_map/all_to_all | solution.py:88
  74.6 0.8 reduce.19
  77.6 1.5 fusion.76
  80.0 1.3 copy.323
  81.3 1.5 fusion.27
  83.8 1.5 multiply_reduce_fusion.3
  85.3 1.6 fusion.16
  86.9 1.3 copy.328
  88.2 1.5 fusion.20
  90.4 1.8 fusion.50
  92.1 1.1 fusion.40
  94.9 1.6 fusion.132
  96.9 1.4 copy.340
  99.0 1.6 pad_add_fusion.1
  100.6 1.1 copy.342
  101.8 1.9 reshape.323
  103.7 4.4 all-to-all-start.3
  108.2 9.8 %all-to-all-done.3 = f32[64,1,256]{2,1,0:T(1,128)S(1)} async-done(((f32[64,1,256]{2,1,0:T(1,128)}), f32[64,1,256]{2,1,0:T(1,128)S(1)}, u32[]{:S(2)}, u32[]{:S(2)}) %all-to-all-start.3) | async-done | bytes 65568 | tf_op jit(solution)/shard_map/all_to_all | solution.py:98
  118.0 0.8 reduce.20
  120.3 1.0 gather_fusion.5
  122.2 67.0 %all-reduce.10.cloned.1.call-done = f32[59,512]{1,0:T(8,128)} async-done(((f32[59,512]{1,0:T(8,128)}), f32[59,512]{1,0:T(8,128)}) %all-reduce.10.cloned.1.call-update) | async-done | bytes 120848 | tf_op jit(solution)/shard_map/psum | solution.py:109
  189.3 1.6 multiply_reduce_fusion.6
  190.9 130.7 %all-reduce.6 = (f32[]{:T(128)}, f32[]{:T(128)}) all-reduce(f32[]{:T(128)} %get-tuple-element.32, f32[]{:T(128)} %get-tuple-element.31), channel_id=1, replica_groups=mesh['views'=8,'tiles'=64] {'tiles'}, use_global_device_ids=true, to_apply=%region_1.0 | all-reduce | flops 2 | bytes 16 | tf_op jit(solution)/shard_map/psum | solution.py:102
  323.7 124.1 %psum.45 = f32[]{:T(128)} all-reduce(f32[]{:T(128)} %get-tuple-element.35), channel_id=1, replica_groups=mesh['views'=8,'tiles'=64] {'tiles'}, use_global_device_ids=true, to_apply=%region_19.25 | all-reduce | flops 1 | bytes 8 | tf_op jit(solution)/shard_map/psum | solution.py:102
  449.7 1.0 gather_fusion.6
  451.8 0.8 gather_fusion.7
  452.6 1.1 fusion.134
  453.7 1.3 reshape.325
  455.0 14.4 %all_to_all.39 = f32[64,1,256]{2,1,0:T(1,128)S(1)} all-to-all(f32[64,1,256]{2,1,0:T(1,128)S(1)} %reshape.325), channel_id=1, replica_groups=mesh['views'=8,'tiles'=64] {'tiles'}, dimensions={0} | all-to-all | bytes 131072 | tf_op jit(solution)/shard_map/all_to_all | solution.py:88
  469.3 0.8 reduce.21
  470.3 1.0 slice.73
  471.3 1.5 fusion.25
  473.0 2.9 fusion.77
  475.8 1.6 copy.357
  477.4 1.1 fusion.21
  478.7 1.6 fusion.15
  480.2 1.3 copy.354
  481.5 1.5 fusion.19
  483.0 1.0 fusion.47
  484.3 1.1 fusion.44
  486.1 0.8 fusion.133
  488.8 13.6 %all_to_all.40 = f32[64,1,256]{2,1,0:T(1,128)S(1)} all-to-all(f32[64,1,256]{2,1,0:T(1,128)S(1)} %reshape.327), channel_id=1, replica_groups=mesh['views'=8,'tiles'=64] {'tiles'}, dimensions={0} | all-to-all | bytes 131072 | tf_op jit(solution)/shard_map/all_to_all | solution.py:98
  502.4 0.8 reduce.22
  504.7 1.0 gather_fusion.9
  506.5 64.2 %all-reduce.12.cloned.1.call-done = f32[59,512]{1,0:T(8,128)} async-done(((f32[59,512]{1,0:T(8,128)}), f32[59,512]{1,0:T(8,128)}) %all-reduce.12.cloned.1.call-update) | async-done | bytes 120848 | tf_op jit(solution)/shard_map/psum | solution.py:109
  570.8 1.6 multiply_reduce_fusion.4
  572.4 130.7 %psum.47 = f32[]{:T(128)} all-reduce(f32[]{:T(128)} %multiply_reduce_fusion.4), channel_id=1, replica_groups=mesh['views'=8,'tiles'=64] {'tiles'}, use_global_device_ids=true, to_apply=%region_28.34 | all-reduce | flops 1 | bytes 8 | tf_op jit(solution)/shard_map/psum | solution.py:110
  (130 shorter events, 27.6 us)
Async XLA Ops:
  7.2 26.5 %copy-start = (f32[1,59,16]{1,2,0:T(8,128)S(1)}, f32[1,59,16]{1,2,0:T(8,128)}, u32[]{:S(2)}) copy-start(f32[1,59,16]{1,2,0:T(8,128)} %param.21) | copy-start | bytes 11332
  7.2 0.7 copy-start.19
  7.2 23.2 %copy-start.1 = (f32[59,512]{1,0:T(8,128)S(1)}, f32[59,512]{1,0:T(8,128)}, u32[]{:S(2)}) copy-start(f32[59,512]{1,0:T(8,128)} %param.19) | copy-start | bytes 362500
  10.2 29.9 %all-to-all-start.2 = ((f32[64,2,1]{1,2,0:T(1,128)}), f32[64,2,1]{1,2,0:T(1,128)S(1)}, u32[]{:S(2)}, u32[]{:S(2)}) async-start(f32[64,2,1]{1,2,0:T(1,128)} %bitcast.28), calls=%async_computation.2 | async-start | bytes 65536 | tf_op jit(solution)/shard_map/all_to_all | solution.py:89
  27.2 10.6 %copy-start.15 = (pred[128]{0:T(512)(128)(4,1)}, pred[128]{0:T(512)(128)(4,1)S(1)}, u32[]{:S(2)}) copy-start(pred[128]{0:T(512)(128)(4,1)S(1)} %compare_and_fusion.8) | copy-start | bytes 388
  30.4 0.9 copy-start.11
  37.9 0.5 copy-start.17
  40.1 20.1 %all-to-all-start.1 = ((f32[64,1,256]{2,1,0:T(1,128)}), f32[64,1,256]{2,1,0:T(1,128)S(1)}, u32[]{:S(2)}, u32[]{:S(2)}) async-start(f32[64,1,256]{2,1,0:T(1,128)} %reshape.319), calls=%async_computation.1 | async-start | bytes 131072 | tf_op jit(solution)/shard_map/all_to_all | solution.py:87
  60.2 14.4 %all-to-all-start = ((f32[64,1,256]{2,1,0:T(1,128)}), f32[64,1,256]{2,1,0:T(1,128)S(1)}, u32[]{:S(2)}, u32[]{:S(2)}) async-start(f32[64,1,256]{2,1,0:T(1,128)} %reshape.321), calls=%async_computation | async-start | bytes 131072 | tf_op jit(solution)/shard_map/all_to_all | solution.py:88
  75.8 0.7 copy-start.12
  82.7 0.8 copy-start.10
  89.7 0.7 copy-start.13
  103.7 14.4 %all-to-all-start.3 = ((f32[64,1,256]{2,1,0:T(1,128)}), f32[64,1,256]{2,1,0:T(1,128)S(1)}, u32[]{:S(2)}, u32[]{:S(2)}) async-start(f32[64,1,256]{2,1,0:T(1,128)} %reshape.323), calls=%async_computation.3 | async-start | bytes 131072 | tf_op jit(solution)/shard_map/all_to_all | solution.py:98
  108.1 81.1 %all-reduce.10.cloned.1.call-start = ((), (), s32[]{:S(2)}) async-start(), calls=%async_computation.6 | async-start | bytes 262144 | tf_op jit(solution)/shard_map/psum | solution.py:109
  121.5 67.8 %copy-start.3 = (f32[59,512]{1,0:T(8,128)S(1)}, f32[59,512]{1,0:T(8,128)}, u32[]{:S(2)}) copy-start(f32[59,512]{1,0:T(8,128)} %param.20) | copy-start | bytes 362500
  122.2 67.1 %copy-start.2 = (f32[59,512]{1,0:T(8,128)S(1)}, f32[59,512]{1,0:T(8,128)}, u32[]{:S(2)}) copy-start(f32[59,512]{1,0:T(8,128)} %param.19) | copy-start | bytes 362500
  122.2 448.6 %all-reduce.12.cloned.1.call-start = ((), (), s32[]{:S(2)}) async-start(), calls=%async_computation.7 | async-start | bytes 262144 | tf_op jit(solution)/shard_map/psum | solution.py:109
  189.3 133.7 %copy-start.8 = (f32[59,512]{1,0:T(8,128)S(1)}, f32[59,512]{1,0:T(8,128)}, u32[]{:S(2)}) copy-start(f32[59,512]{1,0:T(8,128)} %all-reduce.10.cloned.1.call-done) | copy-start | bytes 362500
  323.7 125.3 %copy-start.6 = (f32[59,512]{1,0:T(8,128)}, f32[59,512]{1,0:T(8,128)S(1)}, u32[]{:S(2)}) copy-start(f32[59,512]{1,0:T(8,128)S(1)} %get-tuple-element.36) | copy-start | bytes 362500
  449.0 0.7 copy-start.4
  451.8 0.8 copy-start.16
  451.8 0.8 copy-start.18
  481.5 1.5 copy-start.14
  506.5 64.3 %copy-start.5 = (f32[59,512]{1,0:T(8,128)S(1)}, f32[59,512]{1,0:T(8,128)}, u32[]{:S(2)}) copy-start(f32[59,512]{1,0:T(8,128)} %copy-done.4) | copy-start | bytes 362500
  506.5 197.9 %copy-start.7 = (f32[59,512]{1,0:T(8,128)S(1)}, f32[59,512]{1,0:T(8,128)}, u32[]{:S(2)}) copy-start(f32[59,512]{1,0:T(8,128)} %copy-done.6) | copy-start | bytes 362500
  570.8 133.6 %copy-start.9 = (f32[59,512]{1,0:T(8,128)S(1)}, f32[59,512]{1,0:T(8,128)}, u32[]{:S(2)}) copy-start(f32[59,512]{1,0:T(8,128)} %all-reduce.12.cloned.1.call-done) | copy-start | bytes 362500
Sparse Core Ops, SparseCore 0:
  122.3 66.8 all-reduce.9
  506.7 64.0 all-reduce.11
where the time goes:
time: 720 us; the launch traced here: 712 us
  blocking collectives  413 us (57%)
  waiting for transfers between devices  157 us (22%)
  local copies, waits for them, and re-layouts  40.7 us (6%)
  starting transfers between devices  34.6 us (5%)
  other arithmetic  24.1 us (3%)
  matrix products  23.5 us (3%)
  between operations  18.9 us (3%)
    psum x2, blocking collectives, squares(): return lax.psum(jnp.sum(vector * vector), 'tiles')  255 us
    psum x2, waiting for transfers between devices, body(): product = lax.psum(apply_normal(direction), 'views') + damping * direction  131 us
    psum x1, blocking collectives, body(): step_size = norm_now / lax.psum(jnp.sum(direction * product), 'tiles')  131 us
    all_to_all x1, starting transfers between devices, apply_normal(): lax.all_to_all(marks_send, 'tiles', split_axis=0, concat_axis=0, tiled=True)  14.8 us
  transfers between devices with their start and end apart: 6, of which 5 were waited for; matrix products, arithmetic and copies ran while one was open for 2% of the time, Pallas kernels for 0%

commit v1 on v0

v1 whole, which is shorter than its diff:
```python
import jax
import jax.numpy as jnp
from jax import lax
from jax.experimental import pallas as pl
from jax.experimental.pallas import tpu as pltpu
from jax.sharding import PartitionSpec as P

OFFSET = 6.0
PARAMS = 59
FEAT = 16
ROWS = 8
CAP = 2
PIECES = CAP * ROWS
OWNERS = 64
GAUSS = 512
PIX = 128
F32 = jnp.float32
BF16 = jnp.bfloat16

NN = (((1,), (0,)), ((), ()))
NT = (((1,), (1,)), ((), ()))
TN = (((0,), (0,)), ((), ()))


def iota(shape, axis):
    return lax.broadcasted_iota(jnp.int32, shape, axis)


def mm(a, b, dims=NN):
    return lax.dot_general(a, b, dims, preferred_element_type=F32)


def split(x):
    high = x.astype(BF16)
    low = (x - high.astype(F32)).astype(BF16)
    return high, low


def split3(x):
    high = x.astype(BF16)
    rest = x - high.astype(F32)
    mid = rest.astype(BF16)
    low = (rest - mid.astype(F32)).astype(BF16)
    return high, mid, low


def mm3(a, b, dims=NN):
    ah, al = split(a)
    bh, bl = split(b)
    return mm(ah, bh, dims) + mm(al, bh, dims) + mm(ah, bl, dims)


def total(x):
    return jnp.sum(jnp.sum(x, axis=1, keepdims=True), axis=0, keepdims=True)


def lanes(values, rows):
    lane = iota((rows, PIX), 1)
    out = jnp.zeros((rows, PIX), F32)
    for i, value in enumerate(values):
        out = jnp.where(lane == i, value, out)
    return out


def to_message(feats, select):
    stacked = jnp.concatenate(feats, axis=0)
    high, low = split(stacked)
    slots = mm(high, select, NT) + mm(low, select, NT)
    pieces = [slots[:, i * OWNERS : (i + 1) * OWNERS] for i in range(PIECES)]
    return jnp.concatenate(pieces, axis=0).T


def by_column(message, width):
    turned = message.T
    return jnp.concatenate([turned[i * width : (i + 1) * width] for i in range(PIECES)], axis=1)


def begin(point, right, damp, proj, order, dest, depth):
    blocks = dest.shape[1]
    mine = iota((OWNERS, blocks), 0) == dest
    mine_f = jnp.where(mine, 1.0, 0.0)
    earlier = jnp.where(iota((blocks, blocks), 0) < iota((blocks, blocks), 1), 1.0, 0.0)
    count = mm(mine_f.astype(BF16), earlier.astype(BF16))
    owns = [jnp.where(mine & (count == float(s)), 1.0, 0.0) for s in range(CAP)]
    depth_f = depth.astype(F32) + 1.0
    marks = [jnp.sum(own * depth_f, axis=1, keepdims=True) for own in owns]
    own_all = jnp.concatenate(owns, axis=0).astype(BF16)
    here = iota((blocks, GAUSS), 1) // ROWS == iota((blocks, GAUSS), 0)
    number = jnp.where(here, order + 1, 0)
    parts = jnp.concatenate(
        [(number // 16).astype(F32), (number % 16).astype(F32)], axis=0
    ).astype(BF16)
    pick = jnp.where(iota((GAUSS, PIX), 0) % ROWS == iota((GAUSS, PIX), 1), 1.0, 0.0).astype(BF16)
    table = mm(parts, pick).astype(BF16)
    ids = mm(own_all, table[:blocks]) * 16.0 + mm(own_all, table[blocks:])
    columns = (iota((OWNERS, GAUSS), 1) + 1).astype(F32)
    rows = []
    for s in range(CAP):
        for r in range(ROWS):
            chosen = ids[s * OWNERS : (s + 1) * OWNERS, r : r + 1] == columns
            rows.append(jnp.where(chosen, 1.0, 0.0).astype(BF16))
    select = jnp.concatenate(rows, axis=0)
    feats = mm3(proj, jnp.concatenate([point, right], axis=1), TN)
    message = to_message([feats[:, :GAUSS], feats[:, GAUSS:]], select)
    tail = lanes(marks + [total(right * right), total(damp * right * right)], OWNERS)
    return jnp.concatenate([message, tail], axis=1), select


def order_masks(marks):
    side = CAP * OWNERS
    by_row = jnp.broadcast_to(marks, (side, side))
    diagonal = iota((side, side), 0) == iota((side, side), 1)
    by_lane = jnp.sum(jnp.where(diagonal, by_row, 0.0), axis=0, keepdims=True)
    front = jnp.where((by_lane < by_row) & (by_lane > 0.0), 1.0, 0.0)
    behind = jnp.where((by_row < by_lane) & (by_row > 0.0), 1.0, 0.0)
    return front.astype(BF16), behind.astype(BF16)


def ordered_sum(mask, value):
    high, low = split(value)
    return mm(mask, high) + mm(mask, low)


def image_change(prim_cols, tang_cols, weights, slopes):
    wh, wl = split(weights)
    vh, vl = split(slopes)
    th, tl = split(tang_cols)
    ph, plow = split(prim_cols)
    change = mm(th, wh) + mm(tl, wh) + mm(th, wl) + mm(ph, vh) + mm(plow, vh) + mm(ph, vl)
    row = iota((FEAT, PIX), 0)
    return jnp.where((row >= 1) & (row < 4), change, 0.0)


def pull_back(prim_cols, basis, colour, alphas, clears, weights, behind):
    shade = mm3(prim_cols, colour, TN)
    pulls = [weights[i] * shade[i * OWNERS : (i + 1) * OWNERS] for i in range(PIECES)]
    sums = []
    for s in range(CAP):
        acc = pulls[s * ROWS]
        for r in range(1, ROWS):
            acc = acc + pulls[s * ROWS + r]
        sums.append(acc)
    through = ordered_sum(behind, jnp.concatenate(sums, axis=0))
    logits = [None] * PIECES
    for s in range(CAP):
        acc = through[s * OWNERS : (s + 1) * OWNERS]
        for r in reversed(range(ROWS)):
            i = s * ROWS + r
            logits[i] = clears[i] * pulls[i] - alphas[i] * acc
            acc = acc + pulls[i]
    both = jnp.concatenate(
        [jnp.concatenate(logits, axis=0), jnp.concatenate(weights, axis=0)], axis=1
    )
    back = mm3(both, jnp.concatenate([basis, colour], axis=1), NT)
    return back


def as_rows(back):
    return jnp.concatenate([back[i * OWNERS : (i + 1) * OWNERS] for i in range(PIECES)], axis=1)


def slope_terms(tangents, alphas, clears):
    slopes = []
    sums = []
    for s in range(CAP):
        acc = jnp.zeros((OWNERS, PIX), F32)
        for r in range(ROWS):
            i = s * ROWS + r
            slopes.append(clears[i] * tangents[i] + acc)
            acc = acc - alphas[i] * tangents[i]
        sums.append(acc)
    return slopes, jnp.concatenate(sums, axis=0)


def render_first(message, basis12, pixel_weight):
    width = 2 * FEAT
    columns = by_column(message[:, : PIECES * width], width)
    tail = message[:, PIECES * width :]
    totals = jnp.sum(tail, axis=0, keepdims=True)
    basis = full_basis(basis12)
    both = jnp.zeros((FEAT, PIX), F32)
    wide = jnp.concatenate(
        [jnp.concatenate([basis, both], axis=1), jnp.concatenate([both, basis], axis=1)], axis=0
    )
    logits_tangents = mm3(columns, wide, TN)
    front, behind = order_masks(jnp.concatenate([tail[:, 0:1], tail[:, 1:2]], axis=0))
    alphas, clears, plain, tangents, lengths = [], [], [], [], []
    for s in range(CAP):
        open_now = None
        length = None
        for r in range(ROWS):
            i = s * ROWS + r
            block = logits_tangents[i * OWNERS : (i + 1) * OWNERS]
            z = block[:, :PIX] - OFFSET
            tangents.append(block[:, PIX:])
            small = jnp.exp(-jnp.abs(z))
            grown = 1.0 + small
            part = 1.0 / grown
            rest = small * part
            alpha = jnp.where(z >= 0.0, part, rest)
            clear = jnp.where(z >= 0.0, rest, part)
            log_clear = -(jnp.maximum(z, 0.0) + jnp.log(grown))
            alphas.append(alpha)
            clears.append(clear)
            plain.append(alpha if open_now is None else alpha * open_now)
            open_now = clear if open_now is None else open_now * clear
            length = log_clear if length is None else length + log_clear
        lengths.append(length)
    high, mid, low = split3(jnp.concatenate(lengths, axis=0))
    ahead = jnp.exp(mm(front, high) + mm(front, mid) + mm(front, low))
    weights = [
        plain[i] * ahead[(i // ROWS) * OWNERS : (i // ROWS + 1) * OWNERS] for i in range(PIECES)
    ]
    slopes, sums = slope_terms(tangents, alphas, clears)
    ahead_tangent = ordered_sum(front, sums)
    slopes = [
        weights[i]
        * (slopes[i] + ahead_tangent[(i // ROWS) * OWNERS : (i // ROWS + 1) * OWNERS])
        for i in range(PIECES)
    ]
    prim_cols = columns[:FEAT]
    change = image_change(
        prim_cols,
        columns[FEAT:],
        jnp.concatenate(weights, axis=0),
        jnp.concatenate(slopes, axis=0),
    )
    colour = change * pixel_weight
    back = pull_back(prim_cols, basis, colour, alphas, clears, weights, behind)
    out = jnp.concatenate(
        [as_rows(back), lanes([total(colour * change)], OWNERS)], axis=1
    )
    return (
        out,
        jnp.concatenate(alphas, axis=0),
        jnp.concatenate(clears, axis=0),
        jnp.concatenate(weights, axis=0),
        prim_cols,
        front,
        behind,
        change,
        totals,
    )


def full_basis(basis12):
    first = jnp.where(iota((4, PIX), 0) == 0, 1.0, 0.0)
    return jnp.concatenate([first, basis12], axis=0)


def pieces_of(array):
    return [array[i * OWNERS : (i + 1) * OWNERS] for i in range(PIECES)]


def render_again(
    message, basis12, pixel_weight, alphas, clears, weights, prim_cols, front, behind, change0, totals0
):
    columns = by_column(message[:, : PIECES * FEAT], FEAT)
    totals = jnp.sum(message[:, PIECES * FEAT :], axis=0, keepdims=True)
    basis = full_basis(basis12)
    tangents = pieces_of(mm3(columns, basis, TN))
    alphas, clears, weight_list = pieces_of(alphas), pieces_of(clears), pieces_of(weights)
    slopes, sums = slope_terms(tangents, alphas, clears)
    ahead_tangent = ordered_sum(front, sums)
    slopes = [
        weight_list[i]
        * (slopes[i] + ahead_tangent[(i // ROWS) * OWNERS : (i // ROWS + 1) * OWNERS])
        for i in range(PIECES)
    ]
    ratio = totals[:, 0:1] / totals0[:, 2:3]
    change = (
        image_change(prim_cols, columns, weights, jnp.concatenate(slopes, axis=0))
        + ratio * change0
    )
    colour = change * pixel_weight
    back = pull_back(prim_cols, basis, colour, alphas, clears, weight_list, behind)
    out = jnp.concatenate([as_rows(back), lanes([total(colour * change)], OWNERS)], axis=1)
    return out, totals


def collect(message, select, proj):
    columns = by_column(message[:, : PIECES * FEAT], FEAT)
    high, low = split(columns)
    wide = mm(jnp.concatenate([high, low], axis=0), select)
    gathered = wide[:FEAT] + wide[FEAT:]
    tail = jnp.sum(message[:, PIECES * FEAT :], axis=0, keepdims=True)
    turned = jnp.concatenate(
        [proj.T, jnp.broadcast_to(tail[:, 0:1], (FEAT, PIX - PARAMS))], axis=1
    )
    return jnp.concatenate([gathered, turned], axis=1)


def product_of(message, views):
    rows = views * FEAT
    gathered = message[:, :, :GAUSS].reshape(rows, GAUSS)
    turned = message[:, :, GAUSS:].reshape(rows, PIX)
    product = mm3(turned, gathered, TN)[:PARAMS]
    energy = jnp.sum(turned, axis=0, keepdims=True)[:, PARAMS : PARAMS + 1] * (1.0 / FEAT)
    return product, energy


def step_first(message, right, damp, proj, select, totals0):
    product, energy = product_of(message, message.shape[0])
    product = product + damp * right
    step = totals0[:, 2:3] / (energy + totals0[:, 3:4])
    residual = right - step * product
    weighted = damp * residual
    feats = mm3(proj, residual, TN)
    tail = lanes(
        [total(residual * residual), total(weighted * residual), total(weighted * right)], OWNERS
    )
    out = jnp.concatenate([to_message([feats], select), tail], axis=1)
    return out, residual, step


def step_last(message, right, damp, residual, step, totals0, totals1):
    product, energy = product_of(message, message.shape[0])
    ratio = totals1[:, 0:1] / totals0[:, 2:3]
    direction = residual + ratio * right
    product = product + damp * direction
    damped = totals1[:, 1:2] + 2.0 * ratio * totals1[:, 2:3] + ratio * ratio * totals0[:, 3:4]
    step_now = totals1[:, 0:1] / (energy + damped)
    return step * right + step_now * direction, residual - step_now * product


def call(function, outs, *args):
    def kernel(*refs):
        results = function(*[ref[...] for ref in refs[: len(args)]])
        if len(outs) == 1:
            results = (results,) if not isinstance(results, tuple) else results
        for ref, result in zip(refs[len(args) :], results):
            ref[...] = result

    result = pl.pallas_call(
        kernel,
        out_shape=[jax.ShapeDtypeStruct(shape, dtype) for shape, dtype in outs],
        in_specs=[pl.BlockSpec(memory_space=pltpu.VMEM)] * len(args),
        out_specs=[pl.BlockSpec(memory_space=pltpu.VMEM)] * len(outs),
        compiler_params=pltpu.CompilerParams(vmem_limit_bytes=40 * 1024 * 1024),
        name=function.__name__,
    )(*args)
    return result


def body(
    linear_point,
    right_side,
    damping,
    projection,
    pixel_basis,
    pixel_weight,
    depth_order,
    tile_dest,
    block_depth,
):
    proj = projection[0]
    basis = pixel_basis[0, 0]
    weight = pixel_weight[0]
    dest = tile_dest.reshape(1, -1)
    views = lax.axis_size("views")
    rows = PIECES * OWNERS
    slots = CAP * OWNERS

    def over_tiles(message):
        return lax.all_to_all(message, "tiles", split_axis=0, concat_axis=0, tiled=True)

    def over_views(part):
        spread = jnp.broadcast_to(part[None], (views,) + part.shape)
        return lax.all_to_all(spread, "views", split_axis=0, concat_axis=0, tiled=True)

    message, select = call(
        begin,
        [((OWNERS, PIECES * 2 * FEAT + PIX), F32), ((rows, GAUSS), BF16)],
        linear_point, right_side, damping, proj, depth_order[0], dest, block_depth,
    )
    short = ((OWNERS, PIECES * FEAT + PIX), F32)
    message, alphas, clears, weights, prim, front, behind, change, totals0 = call(
        render_first,
        [short]
        + [((rows, PIX), F32)] * 3
        + [((FEAT, rows), F32)]
        + [((slots, slots), BF16)] * 2
        + [((FEAT, PIX), F32), ((1, PIX), F32)],
        over_tiles(message), basis, weight,
    )
    part_shape = ((FEAT, GAUSS + PIX), F32)
    (part,) = call(collect, [part_shape], over_tiles(message), select, proj)
    message, residual, step = call(
        step_first,
        [short, ((PARAMS, GAUSS), F32), ((1, 1), F32)],
        over_views(part), right_side, damping, proj, select, totals0,
    )
    message, totals1 = call(
        render_again,
        [short, ((1, PIX), F32)],
        over_tiles(message), basis, weight, alphas, clears, weights, prim, front, behind, change, totals0,
    )
    (part,) = call(collect, [part_shape], over_tiles(message), select, proj)
    return tuple(
        call(
            step_last,
            [((PARAMS, GAUSS), F32)] * 2,
            over_views(part), right_side, damping, residual, step, totals0, totals1,
        )
    )


def solution(mesh):
    in_specs = (
        P(None, "tiles"),
        P(None, "tiles"),
        P(None, "tiles"),
        P("views", None, None),
        P("views", "tiles", None, None),
        P("views", "tiles", None),
        P("views", "tiles", None),
        P("views", "tiles", None),
        P("views", "tiles"),
    )
    out_specs = (P(None, "tiles"), P(None, "tiles"))
    return jax.shard_map(body, mesh=mesh, in_specs=in_specs, out_specs=out_specs, check_vma=False)
```

time: 720 us -> 125 us (0.17); the launches traced: 712 us -> 125 us
  blocking collectives: 413 us -> 80.1 us
  waiting for transfers between devices: 157 us -> 10.6 us
  local copies, waits for them, and re-layouts: 40.7 us -> 6.1 us
  other arithmetic: 24.1 us -> 0 us
  matrix products: 23.5 us -> 0 us
  starting transfers between devices: 34.6 us -> 15 us
  between operations: 18.9 us -> 0.77 us
  Pallas kernels: 0 us -> 12.2 us
    psum x3 -> x0, blocking collectives: 386 us -> none  [the longest x2 255 us: squares(): return lax.psum(jnp.sum(vector * vector), 'tiles')]
    psum x2 -> x0, waiting for transfers between devices: 131 us -> none  [body(): product = lax.psum(apply_normal(direction), 'views') + damping * direction]
    all_to_all x2 -> x5, blocking collectives: 28 us -> 80.1 us  [the longest x3 45 us: over_tiles(): lax.all_to_all(message, 'tiles', split_axis=0, concat_axis=0, tiled=True)]
    dot_general x24 -> x0, matrix products: 23.5 us -> none  [the longest x9 12.5 us: blend(): jnp.einsum('scr,srp->scp', blocks[:, 1:4, :], alphas * jnp.exp(before), p...]
    all_to_all x4 -> x1, starting transfers between devices: 34.5 us -> 15 us  [over_tiles(): lax.all_to_all(message, 'tiles', split_axis=0, concat_axis=0, tiled=True)]
    all_to_all x4 -> x1, waiting for transfers between devices: 25.6 us -> 10.6 us  [over_tiles(): lax.all_to_all(message, 'tiles', split_axis=0, concat_axis=0, tiled=True)]
    pallas_call x0 -> x7, Pallas kernels: none -> 12.2 us  [call(): pl.pallas_call(kernel, out_shape=[jax.ShapeDtypeStruct(shape, dtype) for...]
    gather x12 -> x0, local copies, waits for them, and re-layouts: 8.97 us -> none  [the longest x3 3.1 us: to_slots(): jnp.take(vector, local_order, axis=1)]
  transfers between devices with their start and end apart: 6 -> 1, of which waited for: 5 -> 1; matrix products, arithmetic and copies ran while one was open for 2% -> 0% of each run, Pallas kernels for 0% -> 0%
where the time goes in v1:
time: 125 us
  blocking collectives  80.1 us (64%)
  starting transfers between devices  15 us (12%)
  Pallas kernels  12.2 us (10%)
  waiting for transfers between devices  10.6 us (8%)
  local copies, waits for them, and re-layouts  6.1 us (5%)
    all_to_all x3, blocking collectives, over_tiles(): lax.all_to_all(message, 'tiles', split_axis=0, concat_axis=0, tiled=True)  45 us
    all_to_all x2, blocking collectives, over_views(): lax.all_to_all(spread, 'views', split_axis=0, concat_axis=0, tiled=True)  35.1 us
    all_to_all x1, starting transfers between devices, over_tiles(): lax.all_to_all(message, 'tiles', split_axis=0, concat_axis=0, tiled=True)  15 us
    pallas_call x7, Pallas kernels, call(): pl.pallas_call(kernel, out_shape=[jax.ShapeDtypeStruct(shape, dtype) for...  12.2 us
    all_to_all x1, waiting for transfers between devices, over_tiles(): lax.all_to_all(message, 'tiles', split_axis=0, concat_axis=0, tiled=True)  10.6 us
    unnamed x26, local copies, waits for them, and re-layouts  4.88 us
  transfers between devices with their start and end apart: 1, of which 1 were waited for; matrix products, arithmetic and copies ran while one was open for 0% of the time, Pallas kernels for 0%

profile of v1, /device:TPU:1, one launch (start us, length us, event | category | flops | bytes accessed | tf_op | source)
XLA Modules:
  0.0 124.7 jit_solution(12529660816852742509)
XLA Ops:
  0.6 0.8 copy.12
  1.4 0.0 copy-start.5
  1.4 0.0 copy-start.7
  1.4 0.0 copy-start.8
  1.4 0.7 copy-done.5
  2.1 0.0 copy-done.7
  2.1 0.0 copy-done.8
  2.1 0.0 copy-start
  2.1 0.9 copy-done
  3.0 0.0 copy-start.2
  3.0 0.9 copy-done.2
  3.9 0.0 copy-start.4
  3.9 0.9 copy-done.4
  4.8 1.4 %begin.1 = (f32[64,640]{1,0:T(8,128)S(1)}, bf16[1024,512]{1,0:T(8,128)(2,1)S(1)}) custom-call(f32[59,512]{1,0:T(8,128)S(1)} %copy-done.4, f32[59,512]{1,0:T(8,128)S(1)} %copy-done, f32[59,512]{1,0:T(8,128)S(1)} %copy-done.2, f32[59,16]{1,0:T(8,128)S(1)} %bitcast.23, s32[1,512]{1,0:T(1,128)S(1)} %bitcast.37, s32[1,64]{1,0:T(1,128)S(1)} %bitcast.40, ...), custom_call_target="tpu_custom_call" | custom-call | tf_op jit(solution)/shard_map/begin/pallas_call | solution.py:334
  6.2 0.8 copy.13
  7.0 0.0 copy-start.9
  7.0 15.0 %all-to-all-start = ((f32[64,1,640]{2,1,0:T(1,128)}), f32[64,1,640]{2,1,0:T(1,128)S(1)}, u32[]{:S(2)}, u32[]{:S(2)}) async-start(f32[64,1,640]{2,1,0:T(1,128)} %copy.13), calls=%async_computation | async-start | bytes 327680 | tf_op jit(solution)/shard_map/all_to_all | solution.py:365
  22.0 0.0 copy-done.9
  22.0 10.6 %all-to-all-done = f32[64,1,640]{2,1,0:T(1,128)S(1)} async-done(((f32[64,1,640]{2,1,0:T(1,128)}), f32[64,1,640]{2,1,0:T(1,128)S(1)}, u32[]{:S(2)}, u32[]{:S(2)}) %all-to-all-start) | async-done | bytes 163872 | tf_op jit(solution)/shard_map/all_to_all | solution.py:365
  32.6 0.0 copy-start.6
  32.6 0.6 copy-done.6
  33.3 3.7 %render_first.1 = (f32[64,384]{1,0:T(8,128)S(1)}, f32[1024,128]{1,0:T(8,128)S(1)}, f32[1024,128]{1,0:T(8,128)S(1)}, f32[1024,128]{1,0:T(8,128)S(1)}, f32[16,1024...) custom-call(f32[64,640]{1,0:T(8,128)S(1)} %bitcast.27, ...), custom_call_target="tpu_custom_call" | custom-call | tf_op jit(solution)/shard_map/render_first/pallas_call | solution.py:334
  37.0 0.1 copy.14
  37.1 15.3 %all_to_all.54 = f32[64,1,384]{2,1,0:T(1,128)S(1)} all-to-all(f32[64,1,384]{2,1,0:T(1,128)S(1)} %copy.14), channel_id=1, replica_groups=mesh['views'=8,'tiles'=64] {'tiles'}, dimensions={0} | all-to-all | bytes 196608 | tf_op jit(solution)/shard_map/all_to_all | solution.py:365
  52.5 0.4 collect.2
  52.9 0.0 copy-start.1
  52.9 0.0 copy-start.3
  52.9 19.5 %all_to_all.55.refs_0_ = f32[8,16,640]{2,1,0:T(8,128)S(1)} all-to-all(f32[8,16,640]{2,1,0:T(8,128)S(1)} %broadcast_in_dim.4), channel_id=1, replica_groups=mesh['views'=8,'tiles'=64] {'views'}, dimensions={0} | all-to-all | bytes 655360 | tf_op jit(solution)/shard_map/all_to_all | solution.py:369
  72.4 0.0 copy-done.1
  72.4 0.0 copy-done.3
  72.4 1.7 %step_first.1 = (f32[64,384]{1,0:T(8,128)S(1)}, f32[59,512]{1,0:T(8,128)S(1)}, f32[1,1]{1,0:T(1,128)}) custom-call(f32[8,16,640]{2,1,0:T(8,128)S(1)} %all_to_all.55.refs_0_, f32[59,512]{1,0:T(8,128)S(1)} %copy-done.1, f32[59,512]{1,0:T(8,128)S(1)} %copy-done.3, f32[59,16]{1,0:T(8,128)S(1)} %bitcast.25, ...), custom_call_target="tpu_custom_call" | custom-call | tf_op jit(solution)/shard_map/step_first/pallas_call | solution.py:334
  74.1 0.1 copy.15
  74.2 15.3 %all_to_all.56 = f32[64,1,384]{2,1,0:T(1,128)S(1)} all-to-all(f32[64,1,384]{2,1,0:T(1,128)S(1)} %copy.15), channel_id=1, replica_groups=mesh['views'=8,'tiles'=64] {'tiles'}, dimensions={0} | all-to-all | bytes 196608 | tf_op jit(solution)/shard_map/all_to_all | solution.py:365
  89.6 2.9 %render_again.1 = (f32[64,384]{1,0:T(8,128)S(1)}, f32[1,128]{1,0:T(1,128)S(1)}) custom-call(f32[64,384]{1,0:T(8,128)S(1)} %bitcast.28, f32[12,128]{1,0:T(8,128)S(1)} %bitcast.36, f32[1,128]{1,0:T(1,128)S(1)} %bitcast.39, f32[1024,128]{1,0:T(8,128)S(1)} %get-tuple-element.23.refs_3_, f32[1024,128]{1,0:T(8,128)S(1)} %get-tuple-element.24.refs_4_, ...), custom_call_target="tpu_custom_call" | custom-call | tf_op jit(solution)/shard_map/render_again/pallas_call | solution.py:334
  92.5 0.1 copy.16
  92.6 14.3 %all_to_all.57 = f32[64,1,384]{2,1,0:T(1,128)S(1)} all-to-all(f32[64,1,384]{2,1,0:T(1,128)S(1)} %copy.16), channel_id=1, replica_groups=mesh['views'=8,'tiles'=64] {'tiles'}, dimensions={0} | all-to-all | bytes 196608 | tf_op jit(solution)/shard_map/all_to_all | solution.py:365
  107.0 0.4 collect.3
  107.4 15.6 %all_to_all.58.refs_0_ = f32[8,16,640]{2,1,0:T(8,128)S(1)} all-to-all(f32[8,16,640]{2,1,0:T(8,128)S(1)} %broadcast_in_dim.5), channel_id=1, replica_groups=mesh['views'=8,'tiles'=64] {'views'}, dimensions={0} | all-to-all | bytes 655360 | tf_op jit(solution)/shard_map/all_to_all | solution.py:369
  123.0 1.7 %step_last.1 = (f32[59,512]{1,0:T(8,128)}, f32[59,512]{1,0:T(8,128)}) custom-call(f32[8,16,640]{2,1,0:T(8,128)S(1)} %all_to_all.58.refs_0_, f32[59,512]{1,0:T(8,128)S(1)} %copy-done.1, f32[59,512]{1,0:T(8,128)S(1)} %copy-done.3, f32[59,512]{1,0:T(8,128)S(1)} %get-tuple-element.31.refs_3_, f32[1,1]{1,0:T(1,128)} %get-tuple-element.32.refs_4_, ...), custom_call_target="tpu_custom_call" | custom-call | tf_op jit(solution)/shard_map/step_last/pallas_call | solution.py:334
  (7 shorter events, 0.1 us)
Async XLA Ops:
  1.4 0.7 copy-start.5
  1.4 0.7 copy-start.7
  1.4 0.7 copy-start.8
  2.1 0.9 copy-start
  3.0 0.9 copy-start.2
  3.9 0.9 copy-start.4
  7.0 15.0 %copy-start.9 = (f32[1,1,12,128]{3,1,2,0:T(1,128)S(1)}, f32[1,1,12,128]{3,1,2,0:T(1,128)}, u32[]{:S(2)}) copy-start(f32[1,1,12,128]{3,1,2,0:T(1,128)} %param.13) | copy-start | bytes 18436
  7.0 25.6 %all-to-all-start = ((f32[64,1,640]{2,1,0:T(1,128)}), f32[64,1,640]{2,1,0:T(1,128)S(1)}, u32[]{:S(2)}, u32[]{:S(2)}) async-start(f32[64,1,640]{2,1,0:T(1,128)} %copy.13), calls=%async_computation | async-start | bytes 327680 | tf_op jit(solution)/shard_map/all_to_all | solution.py:365
  32.6 0.7 copy-start.6
  52.9 19.5 %copy-start.1 = (f32[59,512]{1,0:T(8,128)S(1)}, f32[59,512]{1,0:T(8,128)}, u32[]{:S(2)}) copy-start(f32[59,512]{1,0:T(8,128)} %refs_1_.5) | copy-start | bytes 362500
  52.9 19.5 %copy-start.3 = (f32[59,512]{1,0:T(8,128)S(1)}, f32[59,512]{1,0:T(8,128)}, u32[]{:S(2)}) copy-start(f32[59,512]{1,0:T(8,128)} %refs_2_.5) | copy-start | bytes 362500

commit v2 on v1

--- a/solution.py
+++ b/solution.py
@@ -75,15 +75,13 @@
     return jnp.concatenate([turned[i * width : (i + 1) * width] for i in range(PIECES)], axis=1)
 
 
-def begin(point, right, damp, proj, order, dest, depth):
+def choose(order, dest):
     blocks = dest.shape[1]
     mine = iota((OWNERS, blocks), 0) == dest
     mine_f = jnp.where(mine, 1.0, 0.0)
     earlier = jnp.where(iota((blocks, blocks), 0) < iota((blocks, blocks), 1), 1.0, 0.0)
     count = mm(mine_f.astype(BF16), earlier.astype(BF16))
     owns = [jnp.where(mine & (count == float(s)), 1.0, 0.0) for s in range(CAP)]
-    depth_f = depth.astype(F32) + 1.0
-    marks = [jnp.sum(own * depth_f, axis=1, keepdims=True) for own in owns]
     own_all = jnp.concatenate(owns, axis=0).astype(BF16)
     here = iota((blocks, GAUSS), 1) // ROWS == iota((blocks, GAUSS), 0)
     number = jnp.where(here, order + 1, 0)
@@ -99,11 +97,61 @@
         for r in range(ROWS):
             chosen = ids[s * OWNERS : (s + 1) * OWNERS, r : r + 1] == columns
             rows.append(jnp.where(chosen, 1.0, 0.0).astype(BF16))
-    select = jnp.concatenate(rows, axis=0)
-    feats = mm3(proj, jnp.concatenate([point, right], axis=1), TN)
+    return owns, jnp.concatenate(rows, axis=0)
+
+
+def begin_kernel(
+    point_hbm, right_hbm, damp_hbm, proj_hbm, basis_hbm, weight_hbm, order_hbm, dest_hbm, depth_hbm,
+    message_ref, select_ref, aux_ref, proj_ref,
+    point, right, damp, proj, basis, weight, order, dest, depth, sems,
+):
+    pairs = [
+        (order_hbm, order), (dest_hbm, dest), (depth_hbm, depth), (proj_hbm, proj),
+        (point_hbm, point), (right_hbm, right), (damp_hbm, damp), (basis_hbm, basis), (weight_hbm, weight),
+    ]
+    copies = [pltpu.make_async_copy(a, b, sems.at[i]) for i, (a, b) in enumerate(pairs)]
+    for copy in copies:
+        copy.start()
+    for copy in copies[:3]:
+        copy.wait()
+    owns, select = choose(order[...], dest[...])
+    select_ref[...] = select
+    depth_f = depth[...].astype(F32) + 1.0
+    marks = [jnp.sum(own * depth_f, axis=1, keepdims=True) for own in owns]
+    for copy in copies[3:7]:
+        copy.wait()
+    right_now = right[...]
+    turned = proj[...]
+    proj_ref[...] = jnp.concatenate([turned, jnp.zeros((FEAT, PIX - PARAMS), F32)], axis=1)
+    feats = mm3(turned, jnp.concatenate([point[...], right_now], axis=1))
     message = to_message([feats[:, :GAUSS], feats[:, GAUSS:]], select)
-    tail = lanes(marks + [total(right * right), total(damp * right * right)], OWNERS)
-    return jnp.concatenate([message, tail], axis=1), select
+    squared = right_now * right_now
+    tail = lanes(marks + [total(squared), total(damp[...] * squared)], OWNERS)
+    message_ref[...] = jnp.concatenate([message, tail], axis=1)
+    for copy in copies[7:]:
+        copy.wait()
+    first = jnp.where(iota((4, PIX), 0) == 0, 1.0, 0.0)
+    last = jnp.broadcast_to(weight[...], (8, PIX))
+    aux_ref[...] = jnp.concatenate([first, basis[:, 0, :], last], axis=0)
+
+
+def begin(*args):
+    rows = PIECES * OWNERS
+    return pl.pallas_call(
+        begin_kernel,
+        out_shape=[
+            jax.ShapeDtypeStruct((OWNERS, PIECES * 2 * FEAT + PIX), F32),
+            jax.ShapeDtypeStruct((rows, GAUSS), BF16),
+            jax.ShapeDtypeStruct((FEAT + 8, PIX), F32),
+            jax.ShapeDtypeStruct((FEAT, PIX), F32),
+        ],
+        in_specs=[pl.BlockSpec(memory_space=pltpu.HBM)] * len(args),
+        out_specs=[pl.BlockSpec(memory_space=pltpu.VMEM)] * 4,
+        scratch_shapes=[pltpu.VMEM(x.shape, x.dtype) for x in args]
+        + [pltpu.SemaphoreType.DMA((len(args),))],
+        compiler_params=pltpu.CompilerParams(vmem_limit_bytes=40 * 1024 * 1024),
+        name="begin",
+    )(*[pltpu.with_memory_space_constraint(x, pltpu.HBM) for x in args])
 
 
 def order_masks(marks):
@@ -172,12 +220,12 @@
     return slopes, jnp.concatenate(sums, axis=0)
 
 
-def render_first(message, basis12, pixel_weight):
+def render_first(message, aux):
     width = 2 * FEAT
     columns = by_column(message[:, : PIECES * width], width)
     tail = message[:, PIECES * width :]
     totals = jnp.sum(tail, axis=0, keepdims=True)
-    basis = full_basis(basis12)
+    basis, pixel_weight = aux[:FEAT], aux[FEAT : FEAT + 1]
     both = jnp.zeros((FEAT, PIX), F32)
     wide = jnp.concatenate(
         [jnp.concatenate([basis, both], axis=1), jnp.concatenate([both, basis], axis=1)], axis=0
@@ -243,21 +291,16 @@
     )
 
 
-def full_basis(basis12):
-    first = jnp.where(iota((4, PIX), 0) == 0, 1.0, 0.0)
-    return jnp.concatenate([first, basis12], axis=0)
-
-
 def pieces_of(array):
     return [array[i * OWNERS : (i + 1) * OWNERS] for i in range(PIECES)]
 
 
 def render_again(
-    message, basis12, pixel_weight, alphas, clears, weights, prim_cols, front, behind, change0, totals0
+    message, aux, alphas, clears, weights, prim_cols, front, behind, change0, totals0
 ):
     columns = by_column(message[:, : PIECES * FEAT], FEAT)
     totals = jnp.sum(message[:, PIECES * FEAT :], axis=0, keepdims=True)
-    basis = full_basis(basis12)
+    basis, pixel_weight = aux[:FEAT], aux[FEAT : FEAT + 1]
     tangents = pieces_of(mm3(columns, basis, TN))
     alphas, clears, weight_list = pieces_of(alphas), pieces_of(clears), pieces_of(weights)
     slopes, sums = slope_terms(tangents, alphas, clears)
@@ -284,28 +327,42 @@
     wide = mm(jnp.concatenate([high, low], axis=0), select)
     gathered = wide[:FEAT] + wide[FEAT:]
     tail = jnp.sum(message[:, PIECES * FEAT :], axis=0, keepdims=True)
-    turned = jnp.concatenate(
-        [proj.T, jnp.broadcast_to(tail[:, 0:1], (FEAT, PIX - PARAMS))], axis=1
-    )
-    return jnp.concatenate([gathered, turned], axis=1)
-
-
-def product_of(message, views):
-    rows = views * FEAT
-    gathered = message[:, :, :GAUSS].reshape(rows, GAUSS)
-    turned = message[:, :, GAUSS:].reshape(rows, PIX)
+    turned = jnp.concatenate([proj[:ROWS, : PIX // 2], proj[ROWS:, : PIX // 2]], axis=1)
+    turned = jnp.where(iota((ROWS, PIX), 1) == PIX - 1, tail[:, 0:1], turned)
+    parts = [gathered[:, j : j + PIX] for j in range(0, GAUSS, PIX)]
+    return jnp.concatenate(parts + [turned], axis=0)
+
+
+def product_of(message):
+    views = message.shape[0]
+    count = GAUSS // PIX
+    gathered = jnp.concatenate(
+        [
+            jnp.concatenate(
+                [
+                    message[:, j * FEAT + h : j * FEAT + h + ROWS].reshape(views * ROWS, PIX)
+                    for j in range(count)
+                ],
+                axis=1,
+            )
+            for h in (0, ROWS)
+        ],
+        axis=0,
+    )
+    last = message[:, count * FEAT :].reshape(views * ROWS, PIX)
+    turned = jnp.concatenate([last[:, : PIX // 2], last[:, PIX // 2 :]], axis=0)
     product = mm3(turned, gathered, TN)[:PARAMS]
-    energy = jnp.sum(turned, axis=0, keepdims=True)[:, PARAMS : PARAMS + 1] * (1.0 / FEAT)
+    energy = jnp.sum(last, axis=0, keepdims=True)[:, PIX - 1 :] * (1.0 / ROWS)
     return product, energy
 
 
 def step_first(message, right, damp, proj, select, totals0):
-    product, energy = product_of(message, message.shape[0])
+    product, energy = product_of(message)
     product = product + damp * right
     step = totals0[:, 2:3] / (energy + totals0[:, 3:4])
     residual = right - step * product
     weighted = damp * residual
-    feats = mm3(proj, residual, TN)
+    feats = mm3(proj[:, :PARAMS], residual)
     tail = lanes(
         [total(residual * residual), total(weighted * residual), total(weighted * right)], OWNERS
     )
@@ -314,7 +371,7 @@
 
 
 def step_last(message, right, damp, residual, step, totals0, totals1):
-    product, energy = product_of(message, message.shape[0])
+    product, energy = product_of(message)
     ratio = totals1[:, 0:1] / totals0[:, 2:3]
     direction = residual + ratio * right
     product = product + damp * direction
@@ -353,9 +410,6 @@
     tile_dest,
     block_depth,
 ):
-    proj = projection[0]
-    basis = pixel_basis[0, 0]
-    weight = pixel_weight[0]
     dest = tile_dest.reshape(1, -1)
     views = lax.axis_size("views")
     rows = PIECES * OWNERS
@@ -368,10 +422,9 @@
         spread = jnp.broadcast_to(part[None], (views,) + part.shape)
         return lax.all_to_all(spread, "views", split_axis=0, concat_axis=0, tiled=True)
 
-    message, select = call(
-        begin,
-        [((OWNERS, PIECES * 2 * FEAT + PIX), F32), ((rows, GAUSS), BF16)],
-        linear_point, right_side, damping, proj, depth_order[0], dest, block_depth,
+    message, select, aux, proj = begin(
+        linear_point, right_side, damping, jnp.swapaxes(projection, 1, 2)[0],
+        pixel_basis.reshape(FEAT - 4, 1, PIX), pixel_weight[0], depth_order[0], dest, block_depth,
     )
     short = ((OWNERS, PIECES * FEAT + PIX), F32)
     message, alphas, clears, weights, prim, front, behind, change, totals0 = call(
@@ -381,9 +434,9 @@
         + [((FEAT, rows), F32)]
         + [((slots, slots), BF16)] * 2
         + [((FEAT, PIX), F32), ((1, PIX), F32)],
-        over_tiles(message), basis, weight,
-    )
-    part_shape = ((FEAT, GAUSS + PIX), F32)
+        over_tiles(message), aux,
+    )
+    part_shape = ((GAUSS // PIX * FEAT + ROWS, PIX), F32)
     (part,) = call(collect, [part_shape], over_tiles(message), select, proj)
     message, residual, step = call(
         step_first,
@@ -393,7 +446,7 @@
     message, totals1 = call(
         render_again,
         [short, ((1, PIX), F32)],
-        over_tiles(message), basis, weight, alphas, clears, weights, prim, front, behind, change, totals0,
+        over_tiles(message), aux, alphas, clears, weights, prim, front, behind, change, totals0,
     )
     (part,) = call(collect, [part_shape], over_tiles(message), select, proj)
     return tuple(

time: 125 us -> 119 us (0.952)
  blocking collectives: 80.1 us -> 104 us
  starting transfers between devices: 15 us -> 0 us
  waiting for transfers between devices: 10.6 us -> 0 us
  local copies, waits for them, and re-layouts: 6.1 us -> 0.59 us
    all_to_all x3 -> x4, blocking collectives: 45 us -> 70.1 us  [over_tiles(): lax.all_to_all(message, 'tiles', split_axis=0, concat_axis=0, tiled=True)]
    all_to_all x1 -> x0, starting transfers between devices: 15 us -> none  [over_tiles(): lax.all_to_all(message, 'tiles', split_axis=0, concat_axis=0, tiled=True)]
    all_to_all x1 -> x0, waiting for transfers between devices: 10.6 us -> none  [over_tiles(): lax.all_to_all(message, 'tiles', split_axis=0, concat_axis=0, tiled=True)]
    unnamed x26 -> x8, local copies, waits for them, and re-layouts: 4.88 us -> 0.05 us
    pallas_call x0 -> x1, Pallas kernels: none -> 2.35 us  [begin(): pl.pallas_call(begin_kernel, out_shape=[jax.ShapeDtypeStruct((OWNERS, PIE...]
    pallas_call x7 -> x6, Pallas kernels: 12.2 us -> 10.7 us  [call(): pl.pallas_call(kernel, out_shape=[jax.ShapeDtypeStruct(shape, dtype) for...]
  transfers between devices with their start and end apart: 1 -> 0, of which waited for: 1 -> 0; matrix products, arithmetic and copies ran while one was open for 0% -> 0% of each run, Pallas kernels for 0% -> 0%
where the time goes in v2:
time: 119 us; the launch traced here: 118 us
  blocking collectives  104 us (87%)
  Pallas kernels  13 us (11%)
    all_to_all x4, blocking collectives, over_tiles(): lax.all_to_all(message, 'tiles', split_axis=0, concat_axis=0, tiled=True)  70.1 us
    all_to_all x2, blocking collectives, over_views(): lax.all_to_all(spread, 'views', split_axis=0, concat_axis=0, tiled=True)  33.9 us
    pallas_call x6, Pallas kernels, call(): pl.pallas_call(kernel, out_shape=[jax.ShapeDtypeStruct(shape, dtype) for...  10.7 us

profile of v2, /device:TPU:1, one launch (start us, length us, event | category | flops | bytes accessed | tf_op | source)
XLA Modules:
  0.0 118.4 jit_solution(14098265868154785938)
XLA Ops:
  0.6 2.4 %begin.1 = (f32[64,640]{1,0:T(8,128)S(1)}, bf16[1024,512]{1,0:T(8,128)(2,1)S(1)}, f32[24,128]{1,0:T(8,128)S(1)}, f32[16,128]{1,0:T(8,128)S(1)}) custom-call(f32[59,512]{1,0:T(8,128)} %point_hbm.1, f32[59,512]{1,0:T(8,128)} %refs_1_.3, f32[59,512]{1,0:T(8,128)} %refs_2_.3, f32[16,59]{1,0:T(8,128)} %bitcast.31, f32[12,1,128]{2,1,0:T(1,128)} %bitcast.32, ...), custom_call_target="tpu_custom_call" | custom-call | tf_op jit(solution)/shard_map/begin/pallas_call | solution.py:140
  3.0 0.2 copy.11
  3.2 25.2 %all_to_all.54 = f32[64,1,640]{2,1,0:T(1,128)S(1)} all-to-all(f32[64,1,640]{2,1,0:T(1,128)S(1)} %copy.11), channel_id=1, replica_groups=mesh['views'=8,'tiles'=64] {'tiles'}, dimensions={0} | all-to-all | bytes 327680 | tf_op jit(solution)/shard_map/all_to_all | solution.py:419
  28.4 3.7 %render_first.1 = (f32[64,384]{1,0:T(8,128)S(1)}, f32[1024,128]{1,0:T(8,128)S(1)}, f32[1024,128]{1,0:T(8,128)S(1)}, f32[1024,128]{1,0:T(8,128)S(1)}, f32[16,1024...) custom-call(f32[64,640]{1,0:T(8,128)S(1)} %bitcast.23, ...), custom_call_target="tpu_custom_call" | custom-call | tf_op jit(solution)/shard_map/render_first/pallas_call | solution.py:391
  32.2 0.1 copy.12
  32.3 15.3 %all_to_all.55 = f32[64,1,384]{2,1,0:T(1,128)S(1)} all-to-all(f32[64,1,384]{2,1,0:T(1,128)S(1)} %copy.12), channel_id=1, replica_groups=mesh['views'=8,'tiles'=64] {'tiles'}, dimensions={0} | all-to-all | bytes 196608 | tf_op jit(solution)/shard_map/all_to_all | solution.py:419
  47.6 0.4 collect.2
  48.1 0.0 copy-start
  48.1 0.0 copy-start.1
  48.1 18.9 %all_to_all.56.refs_0_ = f32[8,72,128]{2,1,0:T(8,128)S(1)} all-to-all(f32[8,72,128]{2,1,0:T(8,128)S(1)} %broadcast_in_dim.4), channel_id=1, replica_groups=mesh['views'=8,'tiles'=64] {'views'}, dimensions={0} | all-to-all | bytes 589824 | tf_op jit(solution)/shard_map/all_to_all | solution.py:423
  67.0 0.0 copy-done
  67.0 0.0 copy-done.1
  67.0 1.6 %step_first.1 = (f32[64,384]{1,0:T(8,128)S(1)}, f32[59,512]{1,0:T(8,128)S(1)}, f32[1,1]{1,0:T(1,128)}) custom-call(f32[8,72,128]{2,1,0:T(8,128)S(1)} %all_to_all.56.refs_0_, f32[59,512]{1,0:T(8,128)S(1)} %copy-done, f32[59,512]{1,0:T(8,128)S(1)} %copy-done.1, f32[16,128]{1,0:T(8,128)S(1)} %get-tuple-element.24.refs_2_.refs_3_, ...), custom_call_target="tpu_custom_call" | custom-call | tf_op jit(solution)/shard_map/step_first/pallas_call | solution.py:391
  68.6 0.1 copy.13
  68.7 15.2 %all_to_all.57 = f32[64,1,384]{2,1,0:T(1,128)S(1)} all-to-all(f32[64,1,384]{2,1,0:T(1,128)S(1)} %copy.13), channel_id=1, replica_groups=mesh['views'=8,'tiles'=64] {'tiles'}, dimensions={0} | all-to-all | bytes 196608 | tf_op jit(solution)/shard_map/all_to_all | solution.py:419
  83.9 2.9 %render_again.1 = (f32[64,384]{1,0:T(8,128)S(1)}, f32[1,128]{1,0:T(1,128)S(1)}) custom-call(f32[64,384]{1,0:T(8,128)S(1)} %bitcast.26, f32[24,128]{1,0:T(8,128)S(1)} %get-tuple-element.21.refs_1_, f32[1024,128]{1,0:T(8,128)S(1)} %get-tuple-element.27.refs_2_, f32[1024,128]{1,0:T(8,128)S(1)} %get-tuple-element.28.refs_3_, ...), custom_call_target="tpu_custom_call" | custom-call | tf_op jit(solution)/shard_map/render_again/pallas_call | solution.py:391
  86.8 0.1 copy.14
  87.0 14.3 %all_to_all.58 = f32[64,1,384]{2,1,0:T(1,128)S(1)} all-to-all(f32[64,1,384]{2,1,0:T(1,128)S(1)} %copy.14), channel_id=1, replica_groups=mesh['views'=8,'tiles'=64] {'tiles'}, dimensions={0} | all-to-all | bytes 196608 | tf_op jit(solution)/shard_map/all_to_all | solution.py:419
  101.3 0.4 collect.3
  101.7 15.0 %all_to_all.59.refs_0_ = f32[8,72,128]{2,1,0:T(8,128)S(1)} all-to-all(f32[8,72,128]{2,1,0:T(8,128)S(1)} %broadcast_in_dim.5), channel_id=1, replica_groups=mesh['views'=8,'tiles'=64] {'views'}, dimensions={0} | all-to-all | bytes 589824 | tf_op jit(solution)/shard_map/all_to_all | solution.py:423
  116.8 1.7 %step_last.1 = (f32[59,512]{1,0:T(8,128)}, f32[59,512]{1,0:T(8,128)}) custom-call(f32[8,72,128]{2,1,0:T(8,128)S(1)} %all_to_all.59.refs_0_, f32[59,512]{1,0:T(8,128)S(1)} %copy-done, f32[59,512]{1,0:T(8,128)S(1)} %copy-done.1, f32[59,512]{1,0:T(8,128)S(1)} %get-tuple-element.35.refs_3_, f32[1,1]{1,0:T(1,128)} %get-tuple-element.36.refs_4_, ...), custom_call_target="tpu_custom_call" | custom-call | tf_op jit(solution)/shard_map/step_last/pallas_call | solution.py:391
  (6 shorter events, 0.1 us)
Async XLA Ops:
  48.1 18.9 %copy-start = (f32[59,512]{1,0:T(8,128)S(1)}, f32[59,512]{1,0:T(8,128)}, u32[]{:S(2)}) copy-start(f32[59,512]{1,0:T(8,128)} %refs_1_.3) | copy-start | bytes 362500
  48.1 18.9 %copy-start.1 = (f32[59,512]{1,0:T(8,128)S(1)}, f32[59,512]{1,0:T(8,128)}, u32[]{:S(2)}) copy-start(f32[59,512]{1,0:T(8,128)} %refs_2_.3) | copy-start | bytes 362500

commit v3 on v2

--- a/solution.py
+++ b/solution.py
@@ -36,18 +36,17 @@
     return high, low
 
 
-def split3(x):
-    high = x.astype(BF16)
-    rest = x - high.astype(F32)
-    mid = rest.astype(BF16)
-    low = (rest - mid.astype(F32)).astype(BF16)
-    return high, mid, low
-
-
-def mm3(a, b, dims=NN):
+def mm_short(a, b):
     ah, al = split(a)
     bh, bl = split(b)
-    return mm(ah, bh, dims) + mm(al, bh, dims) + mm(ah, bl, dims)
+    return mm(jnp.concatenate([ah, al, ah], axis=0), jnp.concatenate([bh, bh, bl], axis=0), TN)
+
+
+def project(proj, vectors):
+    tall = jnp.concatenate([vectors, jnp.zeros((PIX // 2 - PARAMS, vectors.shape[1]), F32)], axis=0)
+    ph, pl_ = split(proj)
+    th, tl = split(tall)
+    return mm(jnp.concatenate([ph, pl_, ph], axis=1), jnp.concatenate([th, th, tl], axis=0))
 
 
 def total(x):
@@ -64,8 +63,13 @@
 
 def to_message(feats, select):
     stacked = jnp.concatenate(feats, axis=0)
-    high, low = split(stacked)
-    slots = mm(high, select, NT) + mm(low, select, NT)
+    rows = stacked.shape[0]
+    both = mm(jnp.concatenate(split(stacked), axis=0), select, NT)
+    slots = both[:rows] + both[rows:]
+    return by_owner(slots)
+
+
+def by_owner(slots):
     pieces = [slots[:, i * OWNERS : (i + 1) * OWNERS] for i in range(PIECES)]
     return jnp.concatenate(pieces, axis=0).T
 
@@ -121,9 +125,9 @@
     for copy in copies[3:7]:
         copy.wait()
     right_now = right[...]
-    turned = proj[...]
-    proj_ref[...] = jnp.concatenate([turned, jnp.zeros((FEAT, PIX - PARAMS), F32)], axis=1)
-    feats = mm3(turned, jnp.concatenate([point[...], right_now], axis=1))
+    padded = jnp.concatenate([proj[...], jnp.zeros((FEAT, PIX - PARAMS), F32)], axis=1)
+    proj_ref[...] = padded
+    feats = project(padded[:, : PIX // 2], jnp.concatenate([point[...], right_now], axis=1))
     message = to_message([feats[:, :GAUSS], feats[:, GAUSS:]], select)
     squared = right_now * right_now
     tail = lanes(marks + [total(squared), total(damp[...] * squared)], OWNERS)
@@ -166,21 +170,28 @@
 
 def ordered_sum(mask, value):
     high, low = split(value)
-    return mm(mask, high) + mm(mask, low)
-
-
-def image_change(prim_cols, tang_cols, weights, slopes):
-    wh, wl = split(weights)
-    vh, vl = split(slopes)
-    th, tl = split(tang_cols)
-    ph, plow = split(prim_cols)
-    change = mm(th, wh) + mm(tl, wh) + mm(th, wl) + mm(ph, vh) + mm(plow, vh) + mm(ph, vl)
+    return mm(jnp.concatenate([mask, mask], axis=1), jnp.concatenate([high, low], axis=0))
+
+
+def image_change(columns, both):
+    high, low = split(columns)
+    bh, bl = split(both)
+    main = mm(jnp.concatenate([high, low], axis=0), bh)
+    rest = mm(high, bl)
+    change = (
+        main[FEAT : 2 * FEAT, :PIX]
+        + main[3 * FEAT :, :PIX]
+        + rest[FEAT:, :PIX]
+        + main[:FEAT, PIX:]
+        + main[2 * FEAT : 3 * FEAT, PIX:]
+        + rest[:FEAT, PIX:]
+    )
     row = iota((FEAT, PIX), 0)
     return jnp.where((row >= 1) & (row < 4), change, 0.0)
 
 
 def pull_back(prim_cols, basis, colour, alphas, clears, weights, behind):
-    shade = mm3(prim_cols, colour, TN)
+    shade = mm_short(prim_cols, colour)
     pulls = [weights[i] * shade[i * OWNERS : (i + 1) * OWNERS] for i in range(PIECES)]
     sums = []
     for s in range(CAP):
@@ -199,12 +210,10 @@
     both = jnp.concatenate(
         [jnp.concatenate(logits, axis=0), jnp.concatenate(weights, axis=0)], axis=1
     )
-    back = mm3(both, jnp.concatenate([basis, colour], axis=1), NT)
-    return back
-
-
-def as_rows(back):
-    return jnp.concatenate([back[i * OWNERS : (i + 1) * OWNERS] for i in range(PIECES)], axis=1)
+    high, low = split(both)
+    bh, bl = split(jnp.concatenate([basis, colour], axis=1))
+    main = mm(jnp.concatenate([bh, bl], axis=0), high, NT)
+    return by_owner(main[:FEAT] + main[FEAT:] + mm(bh, low, NT))
 
 
 def slope_terms(tangents, alphas, clears):
@@ -230,7 +239,7 @@
     wide = jnp.concatenate(
         [jnp.concatenate([basis, both], axis=1), jnp.concatenate([both, basis], axis=1)], axis=0
     )
-    logits_tangents = mm3(columns, wide, TN)
+    logits_tangents = mm_short(columns, wide)
     front, behind = order_masks(jnp.concatenate([tail[:, 0:1], tail[:, 1:2]], axis=0))
     alphas, clears, plain, tangents, lengths = [], [], [], [], []
     for s in range(CAP):
@@ -254,8 +263,7 @@
             open_now = clear if open_now is None else open_now * clear
             length = log_clear if length is None else length + log_clear
         lengths.append(length)
-    high, mid, low = split3(jnp.concatenate(lengths, axis=0))
-    ahead = jnp.exp(mm(front, high) + mm(front, mid) + mm(front, low))
+    ahead = jnp.exp(ordered_sum(front, jnp.concatenate(lengths, axis=0)))
     weights = [
         plain[i] * ahead[(i // ROWS) * OWNERS : (i // ROWS + 1) * OWNERS] for i in range(PIECES)
     ]
@@ -268,15 +276,15 @@
     ]
     prim_cols = columns[:FEAT]
     change = image_change(
-        prim_cols,
-        columns[FEAT:],
-        jnp.concatenate(weights, axis=0),
-        jnp.concatenate(slopes, axis=0),
+        columns,
+        jnp.concatenate(
+            [jnp.concatenate(weights, axis=0), jnp.concatenate(slopes, axis=0)], axis=1
+        ),
     )
     colour = change * pixel_weight
     back = pull_back(prim_cols, basis, colour, alphas, clears, weights, behind)
     out = jnp.concatenate(
-        [as_rows(back), lanes([total(colour * change)], OWNERS)], axis=1
+        [back, lanes([total(colour * change)], OWNERS)], axis=1
     )
     return (
         out,
@@ -301,7 +309,7 @@
     columns = by_column(message[:, : PIECES * FEAT], FEAT)
     totals = jnp.sum(message[:, PIECES * FEAT :], axis=0, keepdims=True)
     basis, pixel_weight = aux[:FEAT], aux[FEAT : FEAT + 1]
-    tangents = pieces_of(mm3(columns, basis, TN))
+    tangents = pieces_of(mm_short(columns, basis))
     alphas, clears, weight_list = pieces_of(alphas), pieces_of(clears), pieces_of(weights)
     slopes, sums = slope_terms(tangents, alphas, clears)
     ahead_tangent = ordered_sum(front, sums)
@@ -312,12 +320,15 @@
     ]
     ratio = totals[:, 0:1] / totals0[:, 2:3]
     change = (
-        image_change(prim_cols, columns, weights, jnp.concatenate(slopes, axis=0))
+        image_change(
+            jnp.concatenate([prim_cols, columns], axis=0),
+            jnp.concatenate([weights, jnp.concatenate(slopes, axis=0)], axis=1),
+        )
         + ratio * change0
     )
     colour = change * pixel_weight
     back = pull_back(prim_cols, basis, colour, alphas, clears, weight_list, behind)
-    out = jnp.concatenate([as_rows(back), lanes([total(colour * change)], OWNERS)], axis=1)
+    out = jnp.concatenate([back, lanes([total(colour * change)], OWNERS)], axis=1)
     return out, totals
 
 
@@ -350,8 +361,18 @@
         axis=0,
     )
     last = message[:, count * FEAT :].reshape(views * ROWS, PIX)
-    turned = jnp.concatenate([last[:, : PIX // 2], last[:, PIX // 2 :]], axis=0)
-    product = mm3(turned, gathered, TN)[:PARAMS]
+    turned = jnp.concatenate([last[:, : PIX // 2], last[:, PIX // 2 :]], axis=0).T
+    th, tl = split(turned)
+    wide = jnp.concatenate(
+        [
+            jnp.concatenate([th, th], axis=1),
+            jnp.concatenate([tl, jnp.zeros(tl.shape, BF16)], axis=1),
+        ],
+        axis=0,
+    )
+    product = mm(wide, jnp.concatenate(split(gathered), axis=0))
+    half = PIX // 2
+    product = (product[:half] + product[half:])[:PARAMS]
     energy = jnp.sum(last, axis=0, keepdims=True)[:, PIX - 1 :] * (1.0 / ROWS)
     return product, energy
 
@@ -362,7 +383,7 @@
     step = totals0[:, 2:3] / (energy + totals0[:, 3:4])
     residual = right - step * product
     weighted = damp * residual
-    feats = mm3(proj[:, :PARAMS], residual)
+    feats = project(proj[:, : PIX // 2], residual)
     tail = lanes(
         [total(residual * residual), total(weighted * residual), total(weighted * right)], OWNERS
     )

time: 119 us -> 116 us (0.975)
  Pallas kernels: 13 us -> 10.3 us
    pallas_call x6, Pallas kernels: 10.7 us -> 8.26 us  [call(): pl.pallas_call(kernel, out_shape=[jax.ShapeDtypeStruct(shape, dtype) for...]
where the time goes in v3:
time: 116 us
  blocking collectives  104 us (90%)
  Pallas kernels  10.3 us (9%)
    all_to_all x4, blocking collectives, over_tiles(): lax.all_to_all(message, 'tiles', split_axis=0, concat_axis=0, tiled=True)  70.1 us
    all_to_all x2, blocking collectives, over_views(): lax.all_to_all(spread, 'views', split_axis=0, concat_axis=0, tiled=True)  33.9 us
    pallas_call x6, Pallas kernels, call(): pl.pallas_call(kernel, out_shape=[jax.ShapeDtypeStruct(shape, dtype) for...  8.26 us

profile of v3, /device:TPU:1, one launch (start us, length us, event | category | flops | bytes accessed | tf_op | source)
XLA Modules:
  0.0 115.7 jit_solution(4821358312845555350)
XLA Ops:
  0.6 2.1 %begin.1 = (f32[64,640]{1,0:T(8,128)S(1)}, bf16[1024,512]{1,0:T(8,128)(2,1)S(1)}, f32[24,128]{1,0:T(8,128)S(1)}, f32[16,128]{1,0:T(8,128)S(1)}) custom-call(f32[59,512]{1,0:T(8,128)} %point_hbm.1, f32[59,512]{1,0:T(8,128)} %refs_1_.3, f32[59,512]{1,0:T(8,128)} %refs_2_.3, f32[16,59]{1,0:T(8,128)} %bitcast.31, f32[12,1,128]{2,1,0:T(1,128)} %bitcast.32, ...), custom_call_target="tpu_custom_call" | custom-call | tf_op jit(solution)/shard_map/begin/pallas_call | solution.py:144
  2.7 0.2 copy.11
  2.9 25.2 %all_to_all.54 = f32[64,1,640]{2,1,0:T(1,128)S(1)} all-to-all(f32[64,1,640]{2,1,0:T(1,128)S(1)} %copy.11), channel_id=1, replica_groups=mesh['views'=8,'tiles'=64] {'tiles'}, dimensions={0} | all-to-all | bytes 327680 | tf_op jit(solution)/shard_map/all_to_all | solution.py:440
  28.1 2.5 %render_first.1 = (f32[64,384]{1,0:T(8,128)S(1)}, f32[1024,128]{1,0:T(8,128)S(1)}, f32[1024,128]{1,0:T(8,128)S(1)}, f32[1024,128]{1,0:T(8,128)S(1)}, f32[16,1024...) custom-call(f32[64,640]{1,0:T(8,128)S(1)} %bitcast.23, ...), custom_call_target="tpu_custom_call" | custom-call | tf_op jit(solution)/shard_map/render_first/pallas_call | solution.py:412
  30.6 0.1 copy.12
  30.8 15.3 %all_to_all.55 = f32[64,1,384]{2,1,0:T(1,128)S(1)} all-to-all(f32[64,1,384]{2,1,0:T(1,128)S(1)} %copy.12), channel_id=1, replica_groups=mesh['views'=8,'tiles'=64] {'tiles'}, dimensions={0} | all-to-all | bytes 196608 | tf_op jit(solution)/shard_map/all_to_all | solution.py:440
  46.1 0.4 collect.2
  46.5 0.0 copy-start
  46.6 0.0 copy-start.1
  46.6 18.9 %all_to_all.56.refs_0_ = f32[8,72,128]{2,1,0:T(8,128)S(1)} all-to-all(f32[8,72,128]{2,1,0:T(8,128)S(1)} %broadcast_in_dim.4), channel_id=1, replica_groups=mesh['views'=8,'tiles'=64] {'views'}, dimensions={0} | all-to-all | bytes 589824 | tf_op jit(solution)/shard_map/all_to_all | solution.py:444
  65.5 0.0 copy-done
  65.5 0.0 copy-done.1
  65.5 1.3 %step_first.1 = (f32[64,384]{1,0:T(8,128)S(1)}, f32[59,512]{1,0:T(8,128)S(1)}, f32[1,1]{1,0:T(1,128)}) custom-call(f32[8,72,128]{2,1,0:T(8,128)S(1)} %all_to_all.56.refs_0_, f32[59,512]{1,0:T(8,128)S(1)} %copy-done, f32[59,512]{1,0:T(8,128)S(1)} %copy-done.1, f32[16,128]{1,0:T(8,128)S(1)} %get-tuple-element.24.refs_2_.refs_3_, ...), custom_call_target="tpu_custom_call" | custom-call | tf_op jit(solution)/shard_map/step_first/pallas_call | solution.py:412
  66.8 0.1 copy.13
  66.9 15.2 %all_to_all.57 = f32[64,1,384]{2,1,0:T(1,128)S(1)} all-to-all(f32[64,1,384]{2,1,0:T(1,128)S(1)} %copy.13), channel_id=1, replica_groups=mesh['views'=8,'tiles'=64] {'tiles'}, dimensions={0} | all-to-all | bytes 196608 | tf_op jit(solution)/shard_map/all_to_all | solution.py:440
  82.1 2.0 %render_again.1 = (f32[64,384]{1,0:T(8,128)S(1)}, f32[1,128]{1,0:T(1,128)S(1)}) custom-call(f32[64,384]{1,0:T(8,128)S(1)} %bitcast.26, f32[24,128]{1,0:T(8,128)S(1)} %get-tuple-element.21.refs_1_, f32[1024,128]{1,0:T(8,128)S(1)} %get-tuple-element.27.refs_2_, f32[1024,128]{1,0:T(8,128)S(1)} %get-tuple-element.28.refs_3_, ...), custom_call_target="tpu_custom_call" | custom-call | tf_op jit(solution)/shard_map/render_again/pallas_call | solution.py:412
  84.1 0.1 copy.14
  84.2 14.3 %all_to_all.58 = f32[64,1,384]{2,1,0:T(1,128)S(1)} all-to-all(f32[64,1,384]{2,1,0:T(1,128)S(1)} %copy.14), channel_id=1, replica_groups=mesh['views'=8,'tiles'=64] {'tiles'}, dimensions={0} | all-to-all | bytes 196608 | tf_op jit(solution)/shard_map/all_to_all | solution.py:440
  98.6 0.4 collect.3
  99.0 15.0 %all_to_all.59.refs_0_ = f32[8,72,128]{2,1,0:T(8,128)S(1)} all-to-all(f32[8,72,128]{2,1,0:T(8,128)S(1)} %broadcast_in_dim.5), channel_id=1, replica_groups=mesh['views'=8,'tiles'=64] {'views'}, dimensions={0} | all-to-all | bytes 589824 | tf_op jit(solution)/shard_map/all_to_all | solution.py:444
  114.1 1.7 %step_last.1 = (f32[59,512]{1,0:T(8,128)}, f32[59,512]{1,0:T(8,128)}) custom-call(f32[8,72,128]{2,1,0:T(8,128)S(1)} %all_to_all.59.refs_0_, f32[59,512]{1,0:T(8,128)S(1)} %copy-done, f32[59,512]{1,0:T(8,128)S(1)} %copy-done.1, f32[59,512]{1,0:T(8,128)S(1)} %get-tuple-element.35.refs_3_, f32[1,1]{1,0:T(1,128)} %get-tuple-element.36.refs_4_, ...), custom_call_target="tpu_custom_call" | custom-call | tf_op jit(solution)/shard_map/step_last/pallas_call | solution.py:412
  (6 shorter events, 0.1 us)
Async XLA Ops:
  46.5 18.9 %copy-start = (f32[59,512]{1,0:T(8,128)S(1)}, f32[59,512]{1,0:T(8,128)}, u32[]{:S(2)}) copy-start(f32[59,512]{1,0:T(8,128)} %refs_1_.3) | copy-start | bytes 362500
  46.6 18.9 %copy-start.1 = (f32[59,512]{1,0:T(8,128)S(1)}, f32[59,512]{1,0:T(8,128)}, u32[]{:S(2)}) copy-start(f32[59,512]{1,0:T(8,128)} %refs_2_.3) | copy-start | bytes 362500

commit v4 on v3

--- a/solution.py
+++ b/solution.py
@@ -1,3 +1,5 @@
+import functools
+
 import jax
 import jax.numpy as jnp
 from jax import lax
@@ -131,7 +133,7 @@
     message = to_message([feats[:, :GAUSS], feats[:, GAUSS:]], select)
     squared = right_now * right_now
     tail = lanes(marks + [total(squared), total(damp[...] * squared)], OWNERS)
-    message_ref[...] = jnp.concatenate([message, tail], axis=1)
+    message_ref[:, 0, :] = jnp.concatenate([message, tail], axis=1)
     for copy in copies[7:]:
         copy.wait()
     first = jnp.where(iota((4, PIX), 0) == 0, 1.0, 0.0)
@@ -144,7 +146,7 @@
     return pl.pallas_call(
         begin_kernel,
         out_shape=[
-            jax.ShapeDtypeStruct((OWNERS, PIECES * 2 * FEAT + PIX), F32),
+            jax.ShapeDtypeStruct((OWNERS, 1, PIECES * 2 * FEAT + PIX), F32),
             jax.ShapeDtypeStruct((rows, GAUSS), BF16),
             jax.ShapeDtypeStruct((FEAT + 8, PIX), F32),
             jax.ShapeDtypeStruct((FEAT, PIX), F32),
@@ -332,7 +334,7 @@
     return out, totals
 
 
-def collect(message, select, proj):
+def collect(views, message, select, proj):
     columns = by_column(message[:, : PIECES * FEAT], FEAT)
     high, low = split(columns)
     wide = mm(jnp.concatenate([high, low], axis=0), select)
@@ -341,7 +343,8 @@
     turned = jnp.concatenate([proj[:ROWS, : PIX // 2], proj[ROWS:, : PIX // 2]], axis=1)
     turned = jnp.where(iota((ROWS, PIX), 1) == PIX - 1, tail[:, 0:1], turned)
     parts = [gathered[:, j : j + PIX] for j in range(0, GAUSS, PIX)]
-    return jnp.concatenate(parts + [turned], axis=0)
+    part = jnp.concatenate(parts + [turned], axis=0)
+    return jnp.broadcast_to(part[None], (views,) + part.shape)
 
 
 def product_of(message):
@@ -388,26 +391,53 @@
         [total(residual * residual), total(weighted * residual), total(weighted * right)], OWNERS
     )
     out = jnp.concatenate([to_message([feats], select), tail], axis=1)
-    return out, residual, step
-
-
-def step_last(message, right, damp, residual, step, totals0, totals1):
-    product, energy = product_of(message)
+    return out, residual, jnp.broadcast_to(step, (1, PIX))
+
+
+def finish_kernel(
+    message, right_ref, damp_ref, residual_ref, step, totals0, totals1,
+    solution_hbm, final_hbm, solution, final, sems,
+):
+    product, energy = product_of(message[...])
+    totals0, totals1 = totals0[...], totals1[...]
+    right, residual = right_ref[...], residual_ref[...]
     ratio = totals1[:, 0:1] / totals0[:, 2:3]
     direction = residual + ratio * right
-    product = product + damp * direction
     damped = totals1[:, 1:2] + 2.0 * ratio * totals1[:, 2:3] + ratio * ratio * totals0[:, 3:4]
     step_now = totals1[:, 0:1] / (energy + damped)
-    return step * right + step_now * direction, residual - step_now * product
+    solution[...] = step[:, 0:1] * right + step_now * direction
+    first = pltpu.make_async_copy(solution, solution_hbm, sems.at[0])
+    first.start()
+    final[...] = residual - step_now * (product + damp_ref[...] * direction)
+    second = pltpu.make_async_copy(final, final_hbm, sems.at[1])
+    second.start()
+    first.wait()
+    second.wait()
+
+
+def finish(*args):
+    shape = (PARAMS, GAUSS)
+    return pl.pallas_call(
+        finish_kernel,
+        out_shape=[jax.ShapeDtypeStruct(shape, F32)] * 2,
+        in_specs=[pl.BlockSpec(memory_space=pltpu.VMEM)] * len(args),
+        out_specs=[pl.BlockSpec(memory_space=pltpu.HBM)] * 2,
+        scratch_shapes=[pltpu.VMEM(shape, F32)] * 2 + [pltpu.SemaphoreType.DMA((2,))],
+        compiler_params=pltpu.CompilerParams(vmem_limit_bytes=40 * 1024 * 1024),
+        name="finish",
+    )(*args)
 
 
 def call(function, outs, *args):
     def kernel(*refs):
-        results = function(*[ref[...] for ref in refs[: len(args)]])
+        results = function(*[ref[:, 0, :] if len(ref.shape) == 3 and ref.shape[1] == 1 else ref[...] for ref in refs[: len(args)]])
         if len(outs) == 1:
             results = (results,) if not isinstance(results, tuple) else results
         for ref, result in zip(refs[len(args) :], results):
-            ref[...] = result
+            if result.ndim == 2 and len(ref.shape) == 3:
+                ref[:, 0, :] = result
+            else:
+                ref[...] = result
 
     result = pl.pallas_call(
         kernel,
@@ -440,14 +470,13 @@
         return lax.all_to_all(message, "tiles", split_axis=0, concat_axis=0, tiled=True)
 
     def over_views(part):
-        spread = jnp.broadcast_to(part[None], (views,) + part.shape)
-        return lax.all_to_all(spread, "views", split_axis=0, concat_axis=0, tiled=True)
+        return lax.all_to_all(part, "views", split_axis=0, concat_axis=0, tiled=True)
 
     message, select, aux, proj = begin(
         linear_point, right_side, damping, jnp.swapaxes(projection, 1, 2)[0],
         pixel_basis.reshape(FEAT - 4, 1, PIX), pixel_weight[0], depth_order[0], dest, block_depth,
     )
-    short = ((OWNERS, PIECES * FEAT + PIX), F32)
+    short = ((OWNERS, 1, PIECES * FEAT + PIX), F32)
     message, alphas, clears, weights, prim, front, behind, change, totals0 = call(
         render_first,
         [short]
@@ -457,11 +486,13 @@
         + [((FEAT, PIX), F32), ((1, PIX), F32)],
         over_tiles(message), aux,
     )
-    part_shape = ((GAUSS // PIX * FEAT + ROWS, PIX), F32)
-    (part,) = call(collect, [part_shape], over_tiles(message), select, proj)
+    part_shape = ((views, GAUSS // PIX * FEAT + ROWS, PIX), F32)
+    gather = functools.partial(collect, views)
+    gather.__name__ = "collect"
+    (part,) = call(gather, [part_shape], over_tiles(message), select, proj)
     message, residual, step = call(
         step_first,
-        [short, ((PARAMS, GAUSS), F32), ((1, 1), F32)],
+        [short, ((PARAMS, GAUSS), F32), ((1, PIX), F32)],
         over_views(part), right_side, damping, proj, select, totals0,
     )
     message, totals1 = call(
@@ -469,13 +500,9 @@
         [short, ((1, PIX), F32)],
         over_tiles(message), aux, alphas, clears, weights, prim, front, behind, change, totals0,
     )
-    (part,) = call(collect, [part_shape], over_tiles(message), select, proj)
+    (part,) = call(gather, [part_shape], over_tiles(message), select, proj)
     return tuple(
-        call(
-            step_last,
-            [((PARAMS, GAUSS), F32)] * 2,
-            over_views(part), right_side, damping, residual, step, totals0, totals1,
-        )
+        finish(over_views(part), right_side, damping, residual, step, totals0, totals1)
     )
 
 

time: 116 us -> 115 us (level)
    pallas_call x6 -> x5, Pallas kernels: 8.26 us -> 6.35 us  [call(): pl.pallas_call(kernel, out_shape=[jax.ShapeDtypeStruct(shape, dtype) for...]
    pallas_call x1 -> x2, Pallas kernels: 2.08 us -> 3.21 us  [the longest x1 2.09 us: begin(): pl.pallas_call(begin_kernel, out_shape=[jax.ShapeDtypeStruct((OWNERS, 1,...]
where the time goes in v4:
time: 115 us; the launch traced here: 114 us
  blocking collectives  104 us (90%)
  Pallas kernels  9.56 us (8%)
    all_to_all x4, blocking collectives, over_tiles(): lax.all_to_all(message, 'tiles', split_axis=0, concat_axis=0, tiled=True)  70.1 us
    all_to_all x2, blocking collectives, over_views(): lax.all_to_all(part, 'views', split_axis=0, concat_axis=0, tiled=True)  33.9 us
    pallas_call x5, Pallas kernels, call(): pl.pallas_call(kernel, out_shape=[jax.ShapeDtypeStruct(shape, dtype) for...  6.35 us

profile of v4, /device:TPU:1, one launch (start us, length us, event | category | flops | bytes accessed | tf_op | source)
XLA Modules:
  0.0 114.3 jit_solution(8577672359500422372)
XLA Ops:
  0.6 2.1 %begin.1 = (f32[64,1,640]{2,1,0:T(1,128)S(1)}, bf16[1024,512]{1,0:T(8,128)(2,1)S(1)}, f32[24,128]{1,0:T(8,128)S(1)}, f32[16,128]{1,0:T(8,128)S(1)}) custom-call(f32[59,512]{1,0:T(8,128)} %point_hbm.1, f32[59,512]{1,0:T(8,128)} %right_ref.1, f32[59,512]{1,0:T(8,128)} %damp_ref.1, f32[16,59]{1,0:T(8,128)} %bitcast.7, f32[12,1,128]{2,1,0:T(1,128)} %bitcast.8, ...), custom_call_target="tpu_custom_call" | custom-call | tf_op jit(solution)/shard_map/begin/pallas_call | solution.py:146
  2.7 25.2 %all_to_all.30.refs_0_ = f32[64,1,640]{2,1,0:T(1,128)S(1)} all-to-all(f32[64,1,640]{2,1,0:T(1,128)S(1)} %get-tuple-element.20), channel_id=1, replica_groups=mesh['views'=8,'tiles'=64] {'tiles'}, dimensions={0} | all-to-all | bytes 327680 | tf_op jit(solution)/shard_map/all_to_all | solution.py:470
  28.0 2.5 %render_first.1 = (f32[64,1,384]{2,1,0:T(1,128)S(1)}, f32[1024,128]{1,0:T(8,128)S(1)}, f32[1024,128]{1,0:T(8,128)S(1)}, f32[1024,128]{1,0:T(8,128)S(1)}, f32[16,...) custom-call(f32[64,1,640]{2,1,0:T(1,128)S(1)} %all_to_all.30.refs_0_, ...), custom_call_target="tpu_custom_call" | custom-call | tf_op jit(solution)/shard_map/render_first/pallas_call | solution.py:442
  30.5 15.3 %all_to_all.31.refs_0_ = f32[64,1,384]{2,1,0:T(1,128)S(1)} all-to-all(f32[64,1,384]{2,1,0:T(1,128)S(1)} %get-tuple-element.22), channel_id=1, replica_groups=mesh['views'=8,'tiles'=64] {'tiles'}, dimensions={0} | all-to-all | bytes 196608 | tf_op jit(solution)/shard_map/all_to_all | solution.py:470
  45.8 0.4 collect.2
  46.3 0.0 copy-start
  46.3 0.0 copy-start.1
  46.3 18.9 %all_to_all.32.refs_0_ = f32[8,72,128]{2,1,0:T(8,128)S(1)} all-to-all(f32[8,72,128]{2,1,0:T(8,128)S(1)} %collect.2), channel_id=1, replica_groups=mesh['views'=8,'tiles'=64] {'views'}, dimensions={0} | all-to-all | bytes 589824 | tf_op jit(solution)/shard_map/all_to_all | solution.py:473
  65.2 0.0 copy-done
  65.2 0.0 copy-done.1
  65.2 0.9 step_first.1
  66.1 15.2 %all_to_all.33.refs_0_ = f32[64,1,384]{2,1,0:T(1,128)S(1)} all-to-all(f32[64,1,384]{2,1,0:T(1,128)S(1)} %get-tuple-element.26), channel_id=1, replica_groups=mesh['views'=8,'tiles'=64] {'tiles'}, dimensions={0} | all-to-all | bytes 196608 | tf_op jit(solution)/shard_map/all_to_all | solution.py:470
  81.4 2.0 %render_again.1 = (f32[64,1,384]{2,1,0:T(1,128)S(1)}, f32[1,128]{1,0:T(1,128)S(1)}) custom-call(f32[64,1,384]{2,1,0:T(1,128)S(1)} %all_to_all.33.refs_0_, f32[24,128]{1,0:T(8,128)S(1)} %get-tuple-element.21.refs_1_, f32[1024,128]{1,0:T(8,128)S(1)} %get-tuple-element.27.refs_2_, f32[1024,128]{1,0:T(8,128)S(1)} %get-tuple-element.28.refs_3_, ...), custom_call_target="tpu_custom_call" | custom-call | tf_op jit(solution)/shard_map/render_again/pallas_call | solution.py:442
  83.4 14.3 %all_to_all.34.refs_0_ = f32[64,1,384]{2,1,0:T(1,128)S(1)} all-to-all(f32[64,1,384]{2,1,0:T(1,128)S(1)} %get-tuple-element.34), channel_id=1, replica_groups=mesh['views'=8,'tiles'=64] {'tiles'}, dimensions={0} | all-to-all | bytes 196608 | tf_op jit(solution)/shard_map/all_to_all | solution.py:470
  97.8 0.4 collect.3
  98.2 15.0 %all_to_all.35.message = f32[8,72,128]{2,1,0:T(8,128)S(1)} all-to-all(f32[8,72,128]{2,1,0:T(8,128)S(1)} %collect.3), channel_id=1, replica_groups=mesh['views'=8,'tiles'=64] {'views'}, dimensions={0} | all-to-all | bytes 589824 | tf_op jit(solution)/shard_map/all_to_all | solution.py:473
  113.2 1.1 finish.1
Async XLA Ops:
  46.3 18.9 %copy-start = (f32[59,512]{1,0:T(8,128)S(1)}, f32[59,512]{1,0:T(8,128)}, u32[]{:S(2)}) copy-start(f32[59,512]{1,0:T(8,128)} %right_ref.1) | copy-start | bytes 362500
  46.3 18.9 %copy-start.1 = (f32[59,512]{1,0:T(8,128)S(1)}, f32[59,512]{1,0:T(8,128)}, u32[]{:S(2)}) copy-start(f32[59,512]{1,0:T(8,128)} %damp_ref.1) | copy-start | bytes 362500

commit v5 on v4

--- a/solution.py
+++ b/solution.py
@@ -97,13 +97,17 @@
     pick = jnp.where(iota((GAUSS, PIX), 0) % ROWS == iota((GAUSS, PIX), 1), 1.0, 0.0).astype(BF16)
     table = mm(parts, pick).astype(BF16)
     ids = mm(own_all, table[:blocks]) * 16.0 + mm(own_all, table[blocks:])
+    return owns, ids
+
+
+def chosen_rows(ids):
     columns = (iota((OWNERS, GAUSS), 1) + 1).astype(F32)
     rows = []
     for s in range(CAP):
         for r in range(ROWS):
             chosen = ids[s * OWNERS : (s + 1) * OWNERS, r : r + 1] == columns
             rows.append(jnp.where(chosen, 1.0, 0.0).astype(BF16))
-    return owns, jnp.concatenate(rows, axis=0)
+    return jnp.concatenate(rows, axis=0)
 
 
 def begin_kernel(
@@ -120,8 +124,7 @@
         copy.start()
     for copy in copies[:3]:
         copy.wait()
-    owns, select = choose(order[...], dest[...])
-    select_ref[...] = select
+    owns, ids = choose(order[...], dest[...])
     depth_f = depth[...].astype(F32) + 1.0
     marks = [jnp.sum(own * depth_f, axis=1, keepdims=True) for own in owns]
     for copy in copies[3:7]:
@@ -130,6 +133,8 @@
     padded = jnp.concatenate([proj[...], jnp.zeros((FEAT, PIX - PARAMS), F32)], axis=1)
     proj_ref[...] = padded
     feats = project(padded[:, : PIX // 2], jnp.concatenate([point[...], right_now], axis=1))
+    select = chosen_rows(ids)
+    select_ref[...] = select
     message = to_message([feats[:, :GAUSS], feats[:, GAUSS:]], select)
     squared = right_now * right_now
     tail = lanes(marks + [total(squared), total(damp[...] * squared)], OWNERS)
@@ -188,6 +193,17 @@
         + main[2 * FEAT : 3 * FEAT, PIX:]
         + rest[:FEAT, PIX:]
     )
+    return colours_only(change)
+
+
+def change_of(columns, values):
+    high, low = split(columns)
+    vh, vl = split(values)
+    main = mm(jnp.concatenate([high, low], axis=0), vh)
+    return main[:FEAT] + main[FEAT:] + mm(high, vl)
+
+
+def colours_only(change):
     row = iota((FEAT, PIX), 0)
     return jnp.where((row >= 1) & (row < 4), change, 0.0)
 
@@ -209,13 +225,14 @@
             i = s * ROWS + r
             logits[i] = clears[i] * pulls[i] - alphas[i] * acc
             acc = acc + pulls[i]
-    both = jnp.concatenate(
-        [jnp.concatenate(logits, axis=0), jnp.concatenate(weights, axis=0)], axis=1
-    )
-    high, low = split(both)
-    bh, bl = split(jnp.concatenate([basis, colour], axis=1))
-    main = mm(jnp.concatenate([bh, bl], axis=0), high, NT)
-    return by_owner(main[:FEAT] + main[FEAT:] + mm(bh, low, NT))
+    def over_pixels(first, second):
+        high, low = split(second)
+        fh, fl = split(first)
+        main = mm(jnp.concatenate([fh, fl], axis=0), high, NT)
+        return main[:FEAT] + main[FEAT:] + mm(fh, low, NT)
+
+    early = over_pixels(colour, jnp.concatenate(weights, axis=0))
+    return by_owner(early + over_pixels(basis, jnp.concatenate(logits, axis=0)))
 
 
 def slope_terms(tangents, alphas, clears):
@@ -322,9 +339,8 @@
     ]
     ratio = totals[:, 0:1] / totals0[:, 2:3]
     change = (
-        image_change(
-            jnp.concatenate([prim_cols, columns], axis=0),
-            jnp.concatenate([weights, jnp.concatenate(slopes, axis=0)], axis=1),
+        colours_only(
+            change_of(columns, weights) + change_of(prim_cols, jnp.concatenate(slopes, axis=0))
         )
         + ratio * change0
     )
@@ -334,36 +350,32 @@
     return out, totals
 
 
-def collect(views, message, select, proj):
+def gathered_parts(message, select):
     columns = by_column(message[:, : PIECES * FEAT], FEAT)
     high, low = split(columns)
     wide = mm(jnp.concatenate([high, low], axis=0), select)
     gathered = wide[:FEAT] + wide[FEAT:]
     tail = jnp.sum(message[:, PIECES * FEAT :], axis=0, keepdims=True)
+    return [gathered[:, j : j + PIX] for j in range(0, GAUSS, PIX)], tail
+
+
+def collect(views, message, select, proj):
+    parts, tail = gathered_parts(message, select)
     turned = jnp.concatenate([proj[:ROWS, : PIX // 2], proj[ROWS:, : PIX // 2]], axis=1)
     turned = jnp.where(iota((ROWS, PIX), 1) == PIX - 1, tail[:, 0:1], turned)
-    parts = [gathered[:, j : j + PIX] for j in range(0, GAUSS, PIX)]
     part = jnp.concatenate(parts + [turned], axis=0)
     return jnp.broadcast_to(part[None], (views,) + part.shape)
 
 
-def product_of(message):
+def collect_last(views, message, select):
+    parts, tail = gathered_parts(message, select)
+    part = jnp.concatenate(parts + [tail], axis=0)
+    return jnp.broadcast_to(part[None], (views,) + part.shape)
+
+
+def turned_pair(message):
     views = message.shape[0]
-    count = GAUSS // PIX
-    gathered = jnp.concatenate(
-        [
-            jnp.concatenate(
-                [
-                    message[:, j * FEAT + h : j * FEAT + h + ROWS].reshape(views * ROWS, PIX)
-                    for j in range(count)
-                ],
-                axis=1,
-            )
-            for h in (0, ROWS)
-        ],
-        axis=0,
-    )
-    last = message[:, count * FEAT :].reshape(views * ROWS, PIX)
+    last = message[:, GAUSS // PIX * FEAT :].reshape(views * ROWS, PIX)
     turned = jnp.concatenate([last[:, : PIX // 2], last[:, PIX // 2 :]], axis=0).T
     th, tl = split(turned)
     wide = jnp.concatenate(
@@ -373,16 +385,33 @@
         ],
         axis=0,
     )
+    energy = jnp.sum(last, axis=0, keepdims=True)[:, PIX - 1 :] * (1.0 / ROWS)
+    return wide, energy
+
+
+def product_of(message, wide):
+    views = message.shape[0]
+    gathered = jnp.concatenate(
+        [
+            jnp.concatenate(
+                [
+                    message[:, j * FEAT + h : j * FEAT + h + ROWS].reshape(views * ROWS, PIX)
+                    for j in range(GAUSS // PIX)
+                ],
+                axis=1,
+            )
+            for h in (0, ROWS)
+        ],
+        axis=0,
+    )
     product = mm(wide, jnp.concatenate(split(gathered), axis=0))
     half = PIX // 2
-    product = (product[:half] + product[half:])[:PARAMS]
-    energy = jnp.sum(last, axis=0, keepdims=True)[:, PIX - 1 :] * (1.0 / ROWS)
-    return product, energy
+    return (product[:half] + product[half:])[:PARAMS]
 
 
 def step_first(message, right, damp, proj, select, totals0):
-    product, energy = product_of(message)
-    product = product + damp * right
+    wide, energy = turned_pair(message)
+    product = product_of(message, wide) + damp * right
     step = totals0[:, 2:3] / (energy + totals0[:, 3:4])
     residual = right - step * product
     weighted = damp * residual
@@ -391,14 +420,16 @@
         [total(residual * residual), total(weighted * residual), total(weighted * right)], OWNERS
     )
     out = jnp.concatenate([to_message([feats], select), tail], axis=1)
-    return out, residual, jnp.broadcast_to(step, (1, PIX))
+    return out, residual, jnp.broadcast_to(step, (1, PIX)), wide
 
 
 def finish_kernel(
-    message, right_ref, damp_ref, residual_ref, step, totals0, totals1,
+    message_ref, right_ref, damp_ref, residual_ref, step, wide, totals0, totals1,
     solution_hbm, final_hbm, solution, final, sems,
 ):
-    product, energy = product_of(message[...])
+    message = message_ref[:, :, 0, :]
+    product = product_of(message, wide[...])
+    energy = jnp.sum(message[:, GAUSS // PIX * FEAT], axis=0, keepdims=True)[:, 0:1]
     totals0, totals1 = totals0[...], totals1[...]
     right, residual = right_ref[...], residual_ref[...]
     ratio = totals1[:, 0:1] / totals0[:, 2:3]
@@ -434,8 +465,8 @@
         if len(outs) == 1:
             results = (results,) if not isinstance(results, tuple) else results
         for ref, result in zip(refs[len(args) :], results):
-            if result.ndim == 2 and len(ref.shape) == 3:
-                ref[:, 0, :] = result
+            if result.ndim < len(ref.shape):
+                ref[..., 0, :] = result
             else:
                 ref[...] = result
 
@@ -490,9 +521,9 @@
     gather = functools.partial(collect, views)
     gather.__name__ = "collect"
     (part,) = call(gather, [part_shape], over_tiles(message), select, proj)
-    message, residual, step = call(
+    message, residual, step, wide = call(
         step_first,
-        [short, ((PARAMS, GAUSS), F32), ((1, PIX), F32)],
+        [short, ((PARAMS, GAUSS), F32), ((1, PIX), F32), ((PIX, 2 * views * FEAT), BF16)],
         over_views(part), right_side, damping, proj, select, totals0,
     )
     message, totals1 = call(
@@ -500,9 +531,12 @@
         [short, ((1, PIX), F32)],
         over_tiles(message), aux, alphas, clears, weights, prim, front, behind, change, totals0,
     )
-    (part,) = call(gather, [part_shape], over_tiles(message), select, proj)
+    gather = functools.partial(collect_last, views)
+    gather.__name__ = "collect_last"
+    last_shape = ((views, GAUSS // PIX * FEAT + 1, 1, PIX), F32)
+    (part,) = call(gather, [last_shape], over_tiles(message), select)
     return tuple(
-        finish(over_views(part), right_side, damping, residual, step, totals0, totals1)
+        finish(over_views(part), right_side, damping, residual, step, wide, totals0, totals1)
     )
 
 

time: 115 us -> 114 us (level)
  no operation moved by 1% of the time
where the time goes in v5:
time: 114 us
  blocking collectives  104 us (91%)
  Pallas kernels  9.24 us (8%)
    all_to_all x4, blocking collectives, over_tiles(): lax.all_to_all(message, 'tiles', split_axis=0, concat_axis=0, tiled=True)  70.2 us
    all_to_all x2, blocking collectives, over_views(): lax.all_to_all(part, 'views', split_axis=0, concat_axis=0, tiled=True)  33.6 us
    pallas_call x5, Pallas kernels, call(): pl.pallas_call(kernel, out_shape=[jax.ShapeDtypeStruct(shape, dtype) for...  6.15 us

profile of v5, /device:TPU:1, one launch (start us, length us, event | category | flops | bytes accessed | tf_op | source)
XLA Modules:
  0.0 113.8 jit_solution(5731129413550619812)
XLA Ops:
  0.6 2.0 %begin.1 = (f32[64,1,640]{2,1,0:T(1,128)S(1)}, bf16[1024,512]{1,0:T(8,128)(2,1)S(1)}, f32[24,128]{1,0:T(8,128)S(1)}, f32[16,128]{1,0:T(8,128)S(1)}) custom-call(f32[59,512]{1,0:T(8,128)} %point_hbm.1, f32[59,512]{1,0:T(8,128)} %right_ref.1, f32[59,512]{1,0:T(8,128)} %damp_ref.1, f32[16,59]{1,0:T(8,128)} %bitcast.7, f32[12,1,128]{2,1,0:T(1,128)} %bitcast.8, ...), custom_call_target="tpu_custom_call" | custom-call | tf_op jit(solution)/shard_map/begin/pallas_call | solution.py:151
  2.6 25.2 %all_to_all.30.refs_0_ = f32[64,1,640]{2,1,0:T(1,128)S(1)} all-to-all(f32[64,1,640]{2,1,0:T(1,128)S(1)} %get-tuple-element.21), channel_id=1, replica_groups=mesh['views'=8,'tiles'=64] {'tiles'}, dimensions={0} | all-to-all | bytes 327680 | tf_op jit(solution)/shard_map/all_to_all | solution.py:501
  27.8 2.4 %render_first.1 = (f32[64,1,384]{2,1,0:T(1,128)S(1)}, f32[1024,128]{1,0:T(8,128)S(1)}, f32[1024,128]{1,0:T(8,128)S(1)}, f32[1024,128]{1,0:T(8,128)S(1)}, f32[16,...) custom-call(f32[64,1,640]{2,1,0:T(1,128)S(1)} %all_to_all.30.refs_0_, ...), custom_call_target="tpu_custom_call" | custom-call | tf_op jit(solution)/shard_map/render_first/pallas_call | solution.py:473
  30.3 15.3 %all_to_all.31.refs_0_ = f32[64,1,384]{2,1,0:T(1,128)S(1)} all-to-all(f32[64,1,384]{2,1,0:T(1,128)S(1)} %get-tuple-element.23), channel_id=1, replica_groups=mesh['views'=8,'tiles'=64] {'tiles'}, dimensions={0} | all-to-all | bytes 196608 | tf_op jit(solution)/shard_map/all_to_all | solution.py:501
  45.6 0.4 collect.1
  46.0 0.0 copy-start
  46.1 0.0 copy-start.1
  46.1 18.9 %all_to_all.32.refs_0_ = f32[8,72,128]{2,1,0:T(8,128)S(1)} all-to-all(f32[8,72,128]{2,1,0:T(8,128)S(1)} %collect.1), channel_id=1, replica_groups=mesh['views'=8,'tiles'=64] {'views'}, dimensions={0} | all-to-all | bytes 589824 | tf_op jit(solution)/shard_map/all_to_all | solution.py:504
  64.9 0.0 copy-done
  64.9 0.0 copy-done.1
  64.9 0.9 step_first.1
  65.9 15.3 %all_to_all.33.refs_0_ = f32[64,1,384]{2,1,0:T(1,128)S(1)} all-to-all(f32[64,1,384]{2,1,0:T(1,128)S(1)} %get-tuple-element.27), channel_id=1, replica_groups=mesh['views'=8,'tiles'=64] {'tiles'}, dimensions={0} | all-to-all | bytes 196608 | tf_op jit(solution)/shard_map/all_to_all | solution.py:501
  81.2 1.8 %render_again.1 = (f32[64,1,384]{2,1,0:T(1,128)S(1)}, f32[1,128]{1,0:T(1,128)S(1)}) custom-call(f32[64,1,384]{2,1,0:T(1,128)S(1)} %all_to_all.33.refs_0_, f32[24,128]{1,0:T(8,128)S(1)} %get-tuple-element.22.refs_1_, f32[1024,128]{1,0:T(8,128)S(1)} %get-tuple-element.28.refs_2_, f32[1024,128]{1,0:T(8,128)S(1)} %get-tuple-element.29.refs_3_, ...), custom_call_target="tpu_custom_call" | custom-call | tf_op jit(solution)/shard_map/render_again/pallas_call | solution.py:473
  83.0 14.3 %all_to_all.34.refs_0_ = f32[64,1,384]{2,1,0:T(1,128)S(1)} all-to-all(f32[64,1,384]{2,1,0:T(1,128)S(1)} %get-tuple-element.35), channel_id=1, replica_groups=mesh['views'=8,'tiles'=64] {'tiles'}, dimensions={0} | all-to-all | bytes 196608 | tf_op jit(solution)/shard_map/all_to_all | solution.py:501
  97.3 0.5 collect_last.1
  97.9 14.8 %all_to_all.35.message_ref = f32[8,65,1,128]{3,2,1,0:T(1,128)S(1)} all-to-all(f32[8,65,1,128]{3,2,1,0:T(1,128)S(1)} %collect_last.1), channel_id=1, replica_groups=mesh['views'=8,'tiles'=64] {'views'}, dimensions={0} | all-to-all | bytes 532480 | tf_op jit(solution)/shard_map/all_to_all | solution.py:504
  112.7 1.1 finish.1
Async XLA Ops:
  46.0 18.9 %copy-start = (f32[59,512]{1,0:T(8,128)S(1)}, f32[59,512]{1,0:T(8,128)}, u32[]{:S(2)}) copy-start(f32[59,512]{1,0:T(8,128)} %right_ref.1) | copy-start | bytes 362500
  46.1 18.9 %copy-start.1 = (f32[59,512]{1,0:T(8,128)S(1)}, f32[59,512]{1,0:T(8,128)}, u32[]{:S(2)}) copy-start(f32[59,512]{1,0:T(8,128)} %damp_ref.1) | copy-start | bytes 362500

commit v6 on v5

--- a/solution.py
+++ b/solution.py
@@ -65,10 +65,11 @@
 
 def to_message(feats, select):
     stacked = jnp.concatenate(feats, axis=0)
+    fields = [slice(i, i + FEAT) for i in range(0, stacked.shape[0], FEAT)]
     rows = stacked.shape[0]
     both = mm(jnp.concatenate(split(stacked), axis=0), select, NT)
     slots = both[:rows] + both[rows:]
-    return by_owner(slots)
+    return jnp.concatenate([by_owner(slots[field]) for field in fields], axis=1)
 
 
 def by_owner(slots):
@@ -111,13 +112,13 @@
 
 
 def begin_kernel(
-    point_hbm, right_hbm, damp_hbm, proj_hbm, basis_hbm, weight_hbm, order_hbm, dest_hbm, depth_hbm,
+    point_hbm, right_hbm, proj_hbm, basis_hbm, weight_hbm, order_hbm, dest_hbm, depth_hbm,
     message_ref, select_ref, aux_ref, proj_ref,
-    point, right, damp, proj, basis, weight, order, dest, depth, sems,
+    point, right, proj, basis, weight, order, dest, depth, sems,
 ):
     pairs = [
         (order_hbm, order), (dest_hbm, dest), (depth_hbm, depth), (proj_hbm, proj),
-        (point_hbm, point), (right_hbm, right), (damp_hbm, damp), (basis_hbm, basis), (weight_hbm, weight),
+        (point_hbm, point), (right_hbm, right), (basis_hbm, basis), (weight_hbm, weight),
     ]
     copies = [pltpu.make_async_copy(a, b, sems.at[i]) for i, (a, b) in enumerate(pairs)]
     for copy in copies:
@@ -127,7 +128,7 @@
     owns, ids = choose(order[...], dest[...])
     depth_f = depth[...].astype(F32) + 1.0
     marks = [jnp.sum(own * depth_f, axis=1, keepdims=True) for own in owns]
-    for copy in copies[3:7]:
+    for copy in copies[3:6]:
         copy.wait()
     right_now = right[...]
     padded = jnp.concatenate([proj[...], jnp.zeros((FEAT, PIX - PARAMS), F32)], axis=1)
@@ -136,10 +137,9 @@
     select = chosen_rows(ids)
     select_ref[...] = select
     message = to_message([feats[:, :GAUSS], feats[:, GAUSS:]], select)
-    squared = right_now * right_now
-    tail = lanes(marks + [total(squared), total(damp[...] * squared)], OWNERS)
+    tail = lanes(marks, OWNERS)
     message_ref[:, 0, :] = jnp.concatenate([message, tail], axis=1)
-    for copy in copies[7:]:
+    for copy in copies[6:]:
         copy.wait()
     first = jnp.where(iota((4, PIX), 0) == 0, 1.0, 0.0)
     last = jnp.broadcast_to(weight[...], (8, PIX))
@@ -208,16 +208,11 @@
     return jnp.where((row >= 1) & (row < 4), change, 0.0)
 
 
-def pull_back(prim_cols, basis, colour, alphas, clears, weights, behind):
+def pull_back(prim_cols, basis, colour, alphas, clears, weights, blended, behind):
     shade = mm_short(prim_cols, colour)
     pulls = [weights[i] * shade[i * OWNERS : (i + 1) * OWNERS] for i in range(PIECES)]
-    sums = []
-    for s in range(CAP):
-        acc = pulls[s * ROWS]
-        for r in range(1, ROWS):
-            acc = acc + pulls[s * ROWS + r]
-        sums.append(acc)
-    through = ordered_sum(behind, jnp.concatenate(sums, axis=0))
+    sums = sum(colour[1 + c : 2 + c] * blended[:, c * PIX : (c + 1) * PIX] for c in range(3))
+    through = ordered_sum(behind, sums)
     logits = [None] * PIECES
     for s in range(CAP):
         acc = through[s * OWNERS : (s + 1) * OWNERS]
@@ -249,10 +244,11 @@
 
 
 def render_first(message, aux):
-    width = 2 * FEAT
-    columns = by_column(message[:, : PIECES * width], width)
-    tail = message[:, PIECES * width :]
-    totals = jnp.sum(tail, axis=0, keepdims=True)
+    width = PIECES * FEAT
+    columns = jnp.concatenate(
+        [by_column(message[:, :width], FEAT), by_column(message[:, width : 2 * width], FEAT)], axis=0
+    )
+    tail = message[:, 2 * width :]
     basis, pixel_weight = aux[:FEAT], aux[FEAT : FEAT + 1]
     both = jnp.zeros((FEAT, PIX), F32)
     wide = jnp.concatenate(
@@ -294,6 +290,25 @@
         for i in range(PIECES)
     ]
     prim_cols = columns[:FEAT]
+    row, lane = iota((FEAT, 3 * PIX), 0), iota((FEAT, 3 * PIX), 1)
+    colours = mm(
+        jnp.concatenate(split(prim_cols), axis=0),
+        jnp.concatenate([jnp.where(row == lane // PIX + 1, 1.0, 0.0).astype(BF16)] * 2, axis=0),
+        TN,
+    )
+    blended = []
+    for c in range(3):
+        shades = pieces_of(colours[:, c * PIX : (c + 1) * PIX])
+        blended.append(
+            jnp.concatenate(
+                [
+                    sum(weights[i] * shades[i] for i in range(s * ROWS, (s + 1) * ROWS))
+                    for s in range(CAP)
+                ],
+                axis=0,
+            )
+        )
+    blended = jnp.concatenate(blended, axis=1)
     change = image_change(
         columns,
         jnp.concatenate(
@@ -301,20 +316,16 @@
         ),
     )
     colour = change * pixel_weight
-    back = pull_back(prim_cols, basis, colour, alphas, clears, weights, behind)
-    out = jnp.concatenate(
-        [back, lanes([total(colour * change)], OWNERS)], axis=1
-    )
+    back = pull_back(prim_cols, basis, colour, alphas, clears, weights, blended, behind)
     return (
-        out,
+        back,
         jnp.concatenate(alphas, axis=0),
         jnp.concatenate(clears, axis=0),
         jnp.concatenate(weights, axis=0),
         prim_cols,
+        blended,
         front,
         behind,
-        change,
-        totals,
     )
 
 
@@ -322,11 +333,31 @@
     return [array[i * OWNERS : (i + 1) * OWNERS] for i in range(PIECES)]
 
 
+def next_direction(message, before):
+    width = PIECES * FEAT
+    tail = message[:, width:]
+    cross, guess, aa, ab, bb, daa, dab, dbb = [tail[:, i : i + 1] for i in range(8)]
+
+    def over_owners(value):
+        return jnp.sum(value, axis=0, keepdims=True)
+
+    start = over_owners(bb)
+    step = start / over_owners(cross)
+    share = step / guess
+    rest = 1.0 - share
+    square = over_owners(share * share * aa + 2.0 * share * rest * ab + rest * rest * bb)
+    ratio = square / start
+    rest = rest + ratio
+    damped = over_owners(share * share * daa + 2.0 * share * rest * dab + rest * rest * dbb)
+    feats = share * message[:, :width] + rest * before[:, width : 2 * width]
+    return feats, lanes([step, ratio, square, damped], 1)
+
+
 def render_again(
-    message, aux, alphas, clears, weights, prim_cols, front, behind, change0, totals0
+    message, before, aux, alphas, clears, weights, prim_cols, blended, front, behind
 ):
-    columns = by_column(message[:, : PIECES * FEAT], FEAT)
-    totals = jnp.sum(message[:, PIECES * FEAT :], axis=0, keepdims=True)
+    feats, scalars = next_direction(message, before)
+    columns = by_column(feats, FEAT)
     basis, pixel_weight = aux[:FEAT], aux[FEAT : FEAT + 1]
     tangents = pieces_of(mm_short(columns, basis))
     alphas, clears, weight_list = pieces_of(alphas), pieces_of(clears), pieces_of(weights)
@@ -337,17 +368,13 @@
         * (slopes[i] + ahead_tangent[(i // ROWS) * OWNERS : (i // ROWS + 1) * OWNERS])
         for i in range(PIECES)
     ]
-    ratio = totals[:, 0:1] / totals0[:, 2:3]
-    change = (
-        colours_only(
-            change_of(columns, weights) + change_of(prim_cols, jnp.concatenate(slopes, axis=0))
-        )
-        + ratio * change0
+    change = colours_only(
+        change_of(columns, weights) + change_of(prim_cols, jnp.concatenate(slopes, axis=0))
     )
     colour = change * pixel_weight
-    back = pull_back(prim_cols, basis, colour, alphas, clears, weight_list, behind)
+    back = pull_back(prim_cols, basis, colour, alphas, clears, weight_list, blended, behind)
     out = jnp.concatenate([back, lanes([total(colour * change)], OWNERS)], axis=1)
-    return out, totals
+    return out, scalars
 
 
 def gathered_parts(message, select):
@@ -355,20 +382,19 @@
     high, low = split(columns)
     wide = mm(jnp.concatenate([high, low], axis=0), select)
     gathered = wide[:FEAT] + wide[FEAT:]
-    tail = jnp.sum(message[:, PIECES * FEAT :], axis=0, keepdims=True)
-    return [gathered[:, j : j + PIX] for j in range(0, GAUSS, PIX)], tail
+    return [gathered[:, j : j + PIX] for j in range(0, GAUSS, PIX)]
 
 
 def collect(views, message, select, proj):
-    parts, tail = gathered_parts(message, select)
+    parts = gathered_parts(message, select)
     turned = jnp.concatenate([proj[:ROWS, : PIX // 2], proj[ROWS:, : PIX // 2]], axis=1)
-    turned = jnp.where(iota((ROWS, PIX), 1) == PIX - 1, tail[:, 0:1], turned)
     part = jnp.concatenate(parts + [turned], axis=0)
     return jnp.broadcast_to(part[None], (views,) + part.shape)
 
 
 def collect_last(views, message, select):
-    parts, tail = gathered_parts(message, select)
+    parts = gathered_parts(message, select)
+    tail = jnp.sum(message[:, PIECES * FEAT :], axis=0, keepdims=True)
     part = jnp.concatenate(parts + [tail], axis=0)
     return jnp.broadcast_to(part[None], (views,) + part.shape)
 
@@ -385,8 +411,7 @@
         ],
         axis=0,
     )
-    energy = jnp.sum(last, axis=0, keepdims=True)[:, PIX - 1 :] * (1.0 / ROWS)
-    return wide, energy
+    return wide
 
 
 def product_of(message, wide):
@@ -409,34 +434,45 @@
     return (product[:half] + product[half:])[:PARAMS]
 
 
-def step_first(message, right, damp, proj, select, totals0):
-    wide, energy = turned_pair(message)
+def step_first(message, right, damp, proj, select):
+    wide = turned_pair(message)
     product = product_of(message, wide) + damp * right
-    step = totals0[:, 2:3] / (energy + totals0[:, 3:4])
-    residual = right - step * product
-    weighted = damp * residual
-    feats = project(proj[:, : PIX // 2], residual)
+    weighted = damp * right
+    bb, dbb = total(right * right), total(weighted * right)
+    cross = total(right * product)
+    guess = jnp.where(bb > 0.0, bb / jnp.maximum(cross, dbb), 1.0)
+    near = right - guess * product
     tail = lanes(
-        [total(residual * residual), total(weighted * residual), total(weighted * right)], OWNERS
-    )
-    out = jnp.concatenate([to_message([feats], select), tail], axis=1)
-    return out, residual, jnp.broadcast_to(step, (1, PIX)), wide
+        [
+            cross,
+            guess,
+            total(near * near),
+            total(near * right),
+            bb,
+            total(damp * near * near),
+            total(weighted * near),
+            dbb,
+        ],
+        OWNERS,
+    )
+    out = jnp.concatenate([to_message([project(proj[:, : PIX // 2], near)], select), tail], axis=1)
+    return out, product, wide
 
 
 def finish_kernel(
-    message_ref, right_ref, damp_ref, residual_ref, step, wide, totals0, totals1,
+    message_ref, right_ref, damp_ref, product_ref, wide, scalars_ref,
     solution_hbm, final_hbm, solution, final, sems,
 ):
     message = message_ref[:, :, 0, :]
     product = product_of(message, wide[...])
     energy = jnp.sum(message[:, GAUSS // PIX * FEAT], axis=0, keepdims=True)[:, 0:1]
-    totals0, totals1 = totals0[...], totals1[...]
-    right, residual = right_ref[...], residual_ref[...]
-    ratio = totals1[:, 0:1] / totals0[:, 2:3]
+    scalars = scalars_ref[...]
+    step, ratio = scalars[:, 0:1], scalars[:, 1:2]
+    right = right_ref[...]
+    residual = right - step * product_ref[...]
     direction = residual + ratio * right
-    damped = totals1[:, 1:2] + 2.0 * ratio * totals1[:, 2:3] + ratio * ratio * totals0[:, 3:4]
-    step_now = totals1[:, 0:1] / (energy + damped)
-    solution[...] = step[:, 0:1] * right + step_now * direction
+    step_now = scalars[:, 2:3] / (energy + scalars[:, 3:4])
+    solution[...] = step * right + step_now * direction
     first = pltpu.make_async_copy(solution, solution_hbm, sems.at[0])
     first.start()
     final[...] = residual - step_now * (product + damp_ref[...] * direction)
@@ -504,39 +540,40 @@
         return lax.all_to_all(part, "views", split_axis=0, concat_axis=0, tiled=True)
 
     message, select, aux, proj = begin(
-        linear_point, right_side, damping, jnp.swapaxes(projection, 1, 2)[0],
+        linear_point, right_side, jnp.swapaxes(projection, 1, 2)[0],
         pixel_basis.reshape(FEAT - 4, 1, PIX), pixel_weight[0], depth_order[0], dest, block_depth,
     )
-    short = ((OWNERS, 1, PIECES * FEAT + PIX), F32)
-    message, alphas, clears, weights, prim, front, behind, change, totals0 = call(
+    width = PIECES * FEAT
+    first_message = over_tiles(message)
+    message, alphas, clears, weights, prim, blended, front, behind = call(
         render_first,
-        [short]
+        [((OWNERS, 1, width), F32)]
         + [((rows, PIX), F32)] * 3
-        + [((FEAT, rows), F32)]
-        + [((slots, slots), BF16)] * 2
-        + [((FEAT, PIX), F32), ((1, PIX), F32)],
-        over_tiles(message), aux,
-    )
+        + [((FEAT, rows), F32), ((slots, 3 * PIX), F32)]
+        + [((slots, slots), BF16)] * 2,
+        first_message, aux,
+    )
+    short = ((OWNERS, 1, width + PIX), F32)
     part_shape = ((views, GAUSS // PIX * FEAT + ROWS, PIX), F32)
     gather = functools.partial(collect, views)
     gather.__name__ = "collect"
     (part,) = call(gather, [part_shape], over_tiles(message), select, proj)
-    message, residual, step, wide = call(
+    message, product, wide = call(
         step_first,
-        [short, ((PARAMS, GAUSS), F32), ((1, PIX), F32), ((PIX, 2 * views * FEAT), BF16)],
-        over_views(part), right_side, damping, proj, select, totals0,
-    )
-    message, totals1 = call(
+        [short, ((PARAMS, GAUSS), F32), ((PIX, 2 * views * FEAT), BF16)],
+        over_views(part), right_side, damping, proj, select,
+    )
+    message, scalars = call(
         render_again,
         [short, ((1, PIX), F32)],
-        over_tiles(message), aux, alphas, clears, weights, prim, front, behind, change, totals0,
+        over_tiles(message), first_message, aux, alphas, clears, weights, prim, blended, front, behind,
     )
     gather = functools.partial(collect_last, views)
     gather.__name__ = "collect_last"
     last_shape = ((views, GAUSS // PIX * FEAT + 1, 1, PIX), F32)
     (part,) = call(gather, [last_shape], over_tiles(message), select)
     return tuple(
-        finish(over_views(part), right_side, damping, residual, step, wide, totals0, totals1)
+        finish(over_views(part), right_side, damping, product, wide, scalars)
     )
 
 

time: 114 us -> 113 us (level)
  no operation moved by 1% of the time
where the time goes in v6:
time: 113 us
  blocking collectives  103 us (91%)
  Pallas kernels  9.15 us (8%)
    all_to_all x4, blocking collectives, over_tiles(): lax.all_to_all(message, 'tiles', split_axis=0, concat_axis=0, tiled=True)  69.5 us
    all_to_all x2, blocking collectives, over_views(): lax.all_to_all(part, 'views', split_axis=0, concat_axis=0, tiled=True)  33.6 us
    pallas_call x5, Pallas kernels, call(): pl.pallas_call(kernel, out_shape=[jax.ShapeDtypeStruct(shape, dtype) for...  6.15 us

profile of v6, /device:TPU:1, one launch (start us, length us, event | category | flops | bytes accessed | tf_op | source)
XLA Modules:
  0.0 113.0 jit_solution(14847200032050417575)
XLA Ops:
  0.6 1.9 %begin.1 = (f32[64,1,640]{2,1,0:T(1,128)S(1)}, bf16[1024,512]{1,0:T(8,128)(2,1)S(1)}, f32[24,128]{1,0:T(8,128)S(1)}, f32[16,128]{1,0:T(8,128)S(1)}) custom-call(f32[59,512]{1,0:T(8,128)} %point_hbm.1, f32[59,512]{1,0:T(8,128)} %right_ref.1, f32[16,59]{1,0:T(8,128)} %bitcast.7, f32[12,1,128]{2,1,0:T(1,128)} %bitcast.8, f32[1,128]{1,0:T(1,128)} %bitcast.10, ...), custom_call_target="tpu_custom_call" | custom-call | tf_op jit(solution)/shard_map/begin/pallas_call | solution.py:151
  2.6 25.2 %all_to_all.30.refs_0_.refs_1_ = f32[64,1,640]{2,1,0:T(1,128)S(1)} all-to-all(f32[64,1,640]{2,1,0:T(1,128)S(1)} %get-tuple-element.19), channel_id=1, replica_groups=mesh['views'=8,'tiles'=64] {'tiles'}, dimensions={0} | all-to-all | bytes 327680 | tf_op jit(solution)/shard_map/all_to_all | solution.py:537
  27.8 2.3 %render_first.1 = (f32[64,1,256]{2,1,0:T(1,128)S(1)}, f32[1024,128]{1,0:T(8,128)S(1)}, f32[1024,128]{1,0:T(8,128)S(1)}, f32[1024,128]{1,0:T(8,128)S(1)}, f32[16,...) custom-call(f32[64,1,640]{2,1,0:T(1,128)S(1)} %all_to_all.30.refs_0_.refs, ...), custom_call_target="tpu_custom_call" | custom-call | tf_op jit(solution)/shard_map/render_first/pallas_call | solution.py:509
  30.1 14.9 %all_to_all.31.refs_0_ = f32[64,1,256]{2,1,0:T(1,128)S(1)} all-to-all(f32[64,1,256]{2,1,0:T(1,128)S(1)} %get-tuple-element.21), channel_id=1, replica_groups=mesh['views'=8,'tiles'=64] {'tiles'}, dimensions={0} | all-to-all | bytes 131072 | tf_op jit(solution)/shard_map/all_to_all | solution.py:537
  45.1 0.4 collect.1
  45.5 0.0 copy-start
  45.5 0.0 copy-start.1
  45.5 18.9 %all_to_all.32.refs_0_ = f32[8,72,128]{2,1,0:T(8,128)S(1)} all-to-all(f32[8,72,128]{2,1,0:T(8,128)S(1)} %collect.1), channel_id=1, replica_groups=mesh['views'=8,'tiles'=64] {'views'}, dimensions={0} | all-to-all | bytes 589824 | tf_op jit(solution)/shard_map/all_to_all | solution.py:540
  64.4 0.0 copy-done
  64.4 0.0 copy-done.1
  64.4 1.0 step_first.1
  65.5 15.0 %all_to_all.33.refs_0_ = f32[64,1,384]{2,1,0:T(1,128)S(1)} all-to-all(f32[64,1,384]{2,1,0:T(1,128)S(1)} %get-tuple-element.24), channel_id=1, replica_groups=mesh['views'=8,'tiles'=64] {'tiles'}, dimensions={0} | all-to-all | bytes 196608 | tf_op jit(solution)/shard_map/all_to_all | solution.py:537
  80.5 1.8 %render_again.1 = (f32[64,1,384]{2,1,0:T(1,128)S(1)}, f32[1,128]{1,0:T(1,128)S(1)}) custom-call(f32[64,1,384]{2,1,0:T(1,128)S(1)} %all_to_all.33.refs_0_, f32[64,1,640]{2,1,0:T(1,128)S(1)} %all_to_all.30.refs_0_.refs_1_, f32[24,128]{1,0:T(8,128)S(1)} %get-tuple-element.20.refs_1_.refs_2_, f32[1024,128]{1,0:T(8,128)S(1)} %get-tuple-element.25.refs_3_, ...), custom_call_target="tpu_custom_call" | custom-call | tf_op jit(solution)/shard_map/render_again/pallas_call | solution.py:509
  82.3 14.3 %all_to_all.34.refs_0_ = f32[64,1,384]{2,1,0:T(1,128)S(1)} all-to-all(f32[64,1,384]{2,1,0:T(1,128)S(1)} %get-tuple-element.32), channel_id=1, replica_groups=mesh['views'=8,'tiles'=64] {'tiles'}, dimensions={0} | all-to-all | bytes 196608 | tf_op jit(solution)/shard_map/all_to_all | solution.py:537
  96.6 0.5 collect_last.1
  97.2 14.8 %all_to_all.35.message_ref = f32[8,65,1,128]{3,2,1,0:T(1,128)S(1)} all-to-all(f32[8,65,1,128]{3,2,1,0:T(1,128)S(1)} %collect_last.1), channel_id=1, replica_groups=mesh['views'=8,'tiles'=64] {'views'}, dimensions={0} | all-to-all | bytes 532480 | tf_op jit(solution)/shard_map/all_to_all | solution.py:540
  112.0 1.0 finish.1
Async XLA Ops:
  45.5 18.9 %copy-start = (f32[59,512]{1,0:T(8,128)S(1)}, f32[59,512]{1,0:T(8,128)}, u32[]{:S(2)}) copy-start(f32[59,512]{1,0:T(8,128)} %right_ref.1) | copy-start | bytes 362500
  45.5 18.9 %copy-start.1 = (f32[59,512]{1,0:T(8,128)S(1)}, f32[59,512]{1,0:T(8,128)}, u32[]{:S(2)}) copy-start(f32[59,512]{1,0:T(8,128)} %damp_ref.1) | copy-start | bytes 362500

commit v7 on v6

--- a/solution.py
+++ b/solution.py
@@ -112,13 +112,13 @@
 
 
 def begin_kernel(
-    point_hbm, right_hbm, proj_hbm, basis_hbm, weight_hbm, order_hbm, dest_hbm, depth_hbm,
+    point_hbm, right_hbm, damp_hbm, proj_hbm, basis_hbm, weight_hbm, order_hbm, dest_hbm, depth_hbm,
     message_ref, select_ref, aux_ref, proj_ref,
-    point, right, proj, basis, weight, order, dest, depth, sems,
+    point, right, damp, proj, basis, weight, order, dest, depth, sems,
 ):
     pairs = [
         (order_hbm, order), (dest_hbm, dest), (depth_hbm, depth), (proj_hbm, proj),
-        (point_hbm, point), (right_hbm, right), (basis_hbm, basis), (weight_hbm, weight),
+        (point_hbm, point), (right_hbm, right), (damp_hbm, damp), (basis_hbm, basis), (weight_hbm, weight),
     ]
     copies = [pltpu.make_async_copy(a, b, sems.at[i]) for i, (a, b) in enumerate(pairs)]
     for copy in copies:
@@ -128,7 +128,7 @@
     owns, ids = choose(order[...], dest[...])
     depth_f = depth[...].astype(F32) + 1.0
     marks = [jnp.sum(own * depth_f, axis=1, keepdims=True) for own in owns]
-    for copy in copies[3:6]:
+    for copy in copies[3:7]:
         copy.wait()
     right_now = right[...]
     padded = jnp.concatenate([proj[...], jnp.zeros((FEAT, PIX - PARAMS), F32)], axis=1)
@@ -137,9 +137,10 @@
     select = chosen_rows(ids)
     select_ref[...] = select
     message = to_message([feats[:, :GAUSS], feats[:, GAUSS:]], select)
-    tail = lanes(marks, OWNERS)
+    squared = right_now * right_now
+    tail = lanes(marks + [total(squared), total(damp[...] * squared)], OWNERS)
     message_ref[:, 0, :] = jnp.concatenate([message, tail], axis=1)
-    for copy in copies[6:]:
+    for copy in copies[7:]:
         copy.wait()
     first = jnp.where(iota((4, PIX), 0) == 0, 1.0, 0.0)
     last = jnp.broadcast_to(weight[...], (8, PIX))
@@ -326,6 +327,7 @@
         blended,
         front,
         behind,
+        jnp.sum(tail, axis=0, keepdims=True),
     )
 
 
@@ -333,31 +335,10 @@
     return [array[i * OWNERS : (i + 1) * OWNERS] for i in range(PIECES)]
 
 
-def next_direction(message, before):
-    width = PIECES * FEAT
-    tail = message[:, width:]
-    cross, guess, aa, ab, bb, daa, dab, dbb = [tail[:, i : i + 1] for i in range(8)]
-
-    def over_owners(value):
-        return jnp.sum(value, axis=0, keepdims=True)
-
-    start = over_owners(bb)
-    step = start / over_owners(cross)
-    share = step / guess
-    rest = 1.0 - share
-    square = over_owners(share * share * aa + 2.0 * share * rest * ab + rest * rest * bb)
-    ratio = square / start
-    rest = rest + ratio
-    damped = over_owners(share * share * daa + 2.0 * share * rest * dab + rest * rest * dbb)
-    feats = share * message[:, :width] + rest * before[:, width : 2 * width]
-    return feats, lanes([step, ratio, square, damped], 1)
-
-
 def render_again(
-    message, before, aux, alphas, clears, weights, prim_cols, blended, front, behind
+    message, own_sums, aux, alphas, clears, weights, prim_cols, blended, front, behind
 ):
-    feats, scalars = next_direction(message, before)
-    columns = by_column(feats, FEAT)
+    columns = by_column(message, FEAT)
     basis, pixel_weight = aux[:FEAT], aux[FEAT : FEAT + 1]
     tangents = pieces_of(mm_short(columns, basis))
     alphas, clears, weight_list = pieces_of(alphas), pieces_of(clears), pieces_of(weights)
@@ -373,8 +354,8 @@
     )
     colour = change * pixel_weight
     back = pull_back(prim_cols, basis, colour, alphas, clears, weight_list, blended, behind)
-    out = jnp.concatenate([back, lanes([total(colour * change)], OWNERS)], axis=1)
-    return out, scalars
+    tail = jnp.where(iota((1, PIX), 1) == 0, total(colour * change), own_sums)
+    return jnp.concatenate([back, jnp.broadcast_to(tail, (OWNERS, PIX))], axis=1)
 
 
 def gathered_parts(message, select):
@@ -434,48 +415,53 @@
     return (product[:half] + product[half:])[:PARAMS]
 
 
-def step_first(message, right, damp, proj, select):
+def first_guess(sums):
+    square, damped = sums[:, 2:3], sums[:, 3:4]
+    return jnp.where(damped > 0.0, square / damped, 1.0)
+
+
+def step_first(message, right, damp, proj, select, start):
     wide = turned_pair(message)
     product = product_of(message, wide) + damp * right
-    weighted = damp * right
-    bb, dbb = total(right * right), total(weighted * right)
-    cross = total(right * product)
-    guess = jnp.where(bb > 0.0, bb / jnp.maximum(cross, dbb), 1.0)
-    near = right - guess * product
-    tail = lanes(
-        [
-            cross,
-            guess,
-            total(near * near),
-            total(near * right),
-            bb,
-            total(damp * near * near),
-            total(weighted * near),
-            dbb,
-        ],
-        OWNERS,
-    )
-    out = jnp.concatenate([to_message([project(proj[:, : PIX // 2], near)], select), tail], axis=1)
-    return out, product, wide
+    near = right - first_guess(start) * product
+    out = to_message([project(proj[:, : PIX // 2], near)], select)
+    sums = [
+        jnp.zeros((1, 1), F32),
+        total(right * product),
+        total(near * near),
+        total(near * right),
+        total(near * product),
+        total(damp * near * near),
+    ]
+    return out, product, wide, lanes(sums, 1)
 
 
 def finish_kernel(
-    message_ref, right_ref, damp_ref, product_ref, wide, scalars_ref,
+    message_ref, right_ref, damp_ref, product_ref, wide, start_ref,
     solution_hbm, final_hbm, solution, final, sems,
 ):
     message = message_ref[:, :, 0, :]
     product = product_of(message, wide[...])
     energy = jnp.sum(message[:, GAUSS // PIX * FEAT], axis=0, keepdims=True)[:, 0:1]
-    scalars = scalars_ref[...]
-    step, ratio = scalars[:, 0:1], scalars[:, 1:2]
-    right = right_ref[...]
-    residual = right - step * product_ref[...]
-    direction = residual + ratio * right
-    step_now = scalars[:, 2:3] / (energy + scalars[:, 3:4])
-    solution[...] = step * right + step_now * direction
+    start = start_ref[...]
+    guess, square = first_guess(start), start[:, 2:3]
+    sums = message[0, GAUSS // PIX * FEAT :]
+    cross, nn, nb, ny, ndn = [sums[:, i : i + 1] for i in range(1, 6)]
+    step = square / cross
+    share = step / guess
+    rest = 1.0 - share
+    square_now = share * share * nn + 2.0 * share * rest * nb + rest * rest * square
+    part = rest + square_now / square
+    bent = share * share * (energy + ndn) + 2.0 * share * part * ny + part * part * cross
+    step_now = square_now / bent
+    right, before = right_ref[...], product_ref[...]
+    near = right - guess * before
+    solution[...] = step * right + step_now * (share * near + part * right)
     first = pltpu.make_async_copy(solution, solution_hbm, sems.at[0])
     first.start()
-    final[...] = residual - step_now * (product + damp_ref[...] * direction)
+    final[...] = (right - step * before) - step_now * (
+        share * (product + damp_ref[...] * near) + part * before
+    )
     second = pltpu.make_async_copy(final, final_hbm, sems.at[1])
     second.start()
     first.wait()
@@ -540,40 +526,44 @@
         return lax.all_to_all(part, "views", split_axis=0, concat_axis=0, tiled=True)
 
     message, select, aux, proj = begin(
-        linear_point, right_side, jnp.swapaxes(projection, 1, 2)[0],
+        linear_point, right_side, damping, jnp.swapaxes(projection, 1, 2)[0],
         pixel_basis.reshape(FEAT - 4, 1, PIX), pixel_weight[0], depth_order[0], dest, block_depth,
     )
     width = PIECES * FEAT
-    first_message = over_tiles(message)
-    message, alphas, clears, weights, prim, blended, front, behind = call(
+    message, alphas, clears, weights, prim, blended, front, behind, start = call(
         render_first,
         [((OWNERS, 1, width), F32)]
         + [((rows, PIX), F32)] * 3
         + [((FEAT, rows), F32), ((slots, 3 * PIX), F32)]
-        + [((slots, slots), BF16)] * 2,
-        first_message, aux,
-    )
-    short = ((OWNERS, 1, width + PIX), F32)
+        + [((slots, slots), BF16)] * 2
+        + [((1, PIX), F32)],
+        over_tiles(message), aux,
+    )
     part_shape = ((views, GAUSS // PIX * FEAT + ROWS, PIX), F32)
     gather = functools.partial(collect, views)
     gather.__name__ = "collect"
     (part,) = call(gather, [part_shape], over_tiles(message), select, proj)
-    message, product, wide = call(
+    message, product, wide, sums = call(
         step_first,
-        [short, ((PARAMS, GAUSS), F32), ((PIX, 2 * views * FEAT), BF16)],
-        over_views(part), right_side, damping, proj, select,
-    )
-    message, scalars = call(
+        [
+            ((OWNERS, 1, width), F32),
+            ((PARAMS, GAUSS), F32),
+            ((PIX, 2 * views * FEAT), BF16),
+            ((1, PIX), F32),
+        ],
+        over_views(part), right_side, damping, proj, select, start,
+    )
+    (message,) = call(
         render_again,
-        [short, ((1, PIX), F32)],
-        over_tiles(message), first_message, aux, alphas, clears, weights, prim, blended, front, behind,
+        [((OWNERS, 1, width + PIX), F32)],
+        over_tiles(message), sums, aux, alphas, clears, weights, prim, blended, front, behind,
     )
     gather = functools.partial(collect_last, views)
     gather.__name__ = "collect_last"
     last_shape = ((views, GAUSS // PIX * FEAT + 1, 1, PIX), F32)
     (part,) = call(gather, [last_shape], over_tiles(message), select)
     return tuple(
-        finish(over_views(part), right_side, damping, product, wide, scalars)
+        finish(over_views(part), right_side, damping, product, wide, start)
     )
 
 

time: 113 us -> 113 us (level)
  no operation moved by 1% of the time
where the time goes in v7:
time: 113 us; the launch traced here: 112 us
  blocking collectives  102 us (90%)
  Pallas kernels  9.06 us (8%)
    all_to_all x4, blocking collectives, over_tiles(): lax.all_to_all(message, 'tiles', split_axis=0, concat_axis=0, tiled=True)  68.8 us
    all_to_all x2, blocking collectives, over_views(): lax.all_to_all(part, 'views', split_axis=0, concat_axis=0, tiled=True)  33.7 us
    pallas_call x5, Pallas kernels, call(): pl.pallas_call(kernel, out_shape=[jax.ShapeDtypeStruct(shape, dtype) for...  5.89 us

profile of v7, /device:TPU:1, one launch (start us, length us, event | category | flops | bytes accessed | tf_op | source)
XLA Modules:
  0.0 112.2 jit_solution(4116251654921485263)
XLA Ops:
  0.6 2.0 %begin.1 = (f32[64,1,640]{2,1,0:T(1,128)S(1)}, bf16[1024,512]{1,0:T(8,128)(2,1)S(1)}, f32[24,128]{1,0:T(8,128)S(1)}, f32[16,128]{1,0:T(8,128)S(1)}) custom-call(f32[59,512]{1,0:T(8,128)} %point_hbm.1, f32[59,512]{1,0:T(8,128)} %right_ref.1, f32[59,512]{1,0:T(8,128)} %damp_ref.1, f32[16,59]{1,0:T(8,128)} %bitcast.7, f32[12,1,128]{2,1,0:T(1,128)} %bitcast.8, ...), custom_call_target="tpu_custom_call" | custom-call | tf_op jit(solution)/shard_map/begin/pallas_call | solution.py:152
  2.7 25.2 %all_to_all.30.refs_0_ = f32[64,1,640]{2,1,0:T(1,128)S(1)} all-to-all(f32[64,1,640]{2,1,0:T(1,128)S(1)} %get-tuple-element.19), channel_id=1, replica_groups=mesh['views'=8,'tiles'=64] {'tiles'}, dimensions={0} | all-to-all | bytes 327680 | tf_op jit(solution)/shard_map/all_to_all | solution.py:523
  27.9 2.3 %render_first.1 = (f32[64,1,256]{2,1,0:T(1,128)S(1)}, f32[1024,128]{1,0:T(8,128)S(1)}, f32[1024,128]{1,0:T(8,128)S(1)}, f32[1024,128]{1,0:T(8,128)S(1)}, f32[16,...) custom-call(f32[64,1,640]{2,1,0:T(1,128)S(1)} %all_to_all.30.refs_0_, ...), custom_call_target="tpu_custom_call" | custom-call | tf_op jit(solution)/shard_map/render_first/pallas_call | solution.py:495
  30.2 14.9 %all_to_all.31.refs_0_ = f32[64,1,256]{2,1,0:T(1,128)S(1)} all-to-all(f32[64,1,256]{2,1,0:T(1,128)S(1)} %get-tuple-element.21), channel_id=1, replica_groups=mesh['views'=8,'tiles'=64] {'tiles'}, dimensions={0} | all-to-all | bytes 131072 | tf_op jit(solution)/shard_map/all_to_all | solution.py:523
  45.2 0.4 collect.1
  45.6 0.0 copy-start
  45.6 0.0 copy-start.1
  45.6 18.9 %all_to_all.32.refs_0_ = f32[8,72,128]{2,1,0:T(8,128)S(1)} all-to-all(f32[8,72,128]{2,1,0:T(8,128)S(1)} %collect.1), channel_id=1, replica_groups=mesh['views'=8,'tiles'=64] {'views'}, dimensions={0} | all-to-all | bytes 589824 | tf_op jit(solution)/shard_map/all_to_all | solution.py:526
  64.5 0.0 copy-done
  64.5 0.0 copy-done.1
  64.5 1.0 step_first.1
  65.6 14.6 %all_to_all.33.refs_0_ = f32[64,1,256]{2,1,0:T(1,128)S(1)} all-to-all(f32[64,1,256]{2,1,0:T(1,128)S(1)} %get-tuple-element.25), channel_id=1, replica_groups=mesh['views'=8,'tiles'=64] {'tiles'}, dimensions={0} | all-to-all | bytes 131072 | tf_op jit(solution)/shard_map/all_to_all | solution.py:523
  80.1 1.6 %render_again.1 = f32[64,1,384]{2,1,0:T(1,128)S(1)} custom-call(f32[64,1,256]{2,1,0:T(1,128)S(1)} %all_to_all.33.refs_0_, f32[1,128]{1,0:T(1,128)S(1)} %get-tuple-element.26.refs_1_, f32[24,128]{1,0:T(8,128)S(1)} %get-tuple-element.20.refs_1_.refs_2_, f32[1024,128]{1,0:T(8,128)S(1)} %get-tuple-element.27.refs_3_, f32[1024,128]{1,0:T(8,128)S(1)} %get-tuple-element.28.refs_4_, ...), custom_call_target="tpu_custom_call" | custom-call | tf_op jit(solution)/shard_map/render_again/pallas_call | solution.py:495
  81.7 14.0 %all_to_all.34.refs_0_ = f32[64,1,384]{2,1,0:T(1,128)S(1)} all-to-all(f32[64,1,384]{2,1,0:T(1,128)S(1)} %render_again.1), channel_id=1, replica_groups=mesh['views'=8,'tiles'=64] {'tiles'}, dimensions={0} | all-to-all | bytes 196608 | tf_op jit(solution)/shard_map/all_to_all | solution.py:523
  95.8 0.5 collect_last.1
  96.3 14.8 %all_to_all.35.message_ref = f32[8,65,1,128]{3,2,1,0:T(1,128)S(1)} all-to-all(f32[8,65,1,128]{3,2,1,0:T(1,128)S(1)} %collect_last.1), channel_id=1, replica_groups=mesh['views'=8,'tiles'=64] {'views'}, dimensions={0} | all-to-all | bytes 532480 | tf_op jit(solution)/shard_map/all_to_all | solution.py:526
  111.1 1.1 %finish.1 = (f32[59,512]{1,0:T(8,128)}, f32[59,512]{1,0:T(8,128)}) custom-call(f32[8,65,1,128]{3,2,1,0:T(1,128)S(1)} %all_to_all.35.message_ref, f32[59,512]{1,0:T(8,128)S(1)} %copy-done, f32[59,512]{1,0:T(8,128)S(1)} %copy-done.1, f32[59,512]{1,0:T(8,128)S(1)} %get-tuple-element.34.product_ref, bf16[128,256]{1,0:T(8,128)(2,1)S(1)} %get-tuple-element.35.wide, ...), custom_call_target="tpu_custom_call" | custom-call | tf_op jit(solution)/shard_map/finish/pallas_call | solution.py:473
Async XLA Ops:
  45.6 18.9 %copy-start = (f32[59,512]{1,0:T(8,128)S(1)}, f32[59,512]{1,0:T(8,128)}, u32[]{:S(2)}) copy-start(f32[59,512]{1,0:T(8,128)} %right_ref.1) | copy-start | bytes 362500
  45.6 18.9 %copy-start.1 = (f32[59,512]{1,0:T(8,128)S(1)}, f32[59,512]{1,0:T(8,128)}, u32[]{:S(2)}) copy-start(f32[59,512]{1,0:T(8,128)} %damp_ref.1) | copy-start | bytes 362500

commit v8 on v7

--- a/solution.py
+++ b/solution.py
@@ -85,15 +85,18 @@
 def choose(order, dest):
     blocks = dest.shape[1]
     mine = iota((OWNERS, blocks), 0) == dest
-    mine_f = jnp.where(mine, 1.0, 0.0)
-    earlier = jnp.where(iota((blocks, blocks), 0) < iota((blocks, blocks), 1), 1.0, 0.0)
-    count = mm(mine_f.astype(BF16), earlier.astype(BF16))
-    owns = [jnp.where(mine & (count == float(s)), 1.0, 0.0) for s in range(CAP)]
+    block = iota((OWNERS, blocks), 1).astype(F32)
+    first = jnp.min(jnp.where(mine, block, float(blocks)), axis=1, keepdims=True)
+    last = jnp.max(jnp.where(mine, block, -1.0), axis=1, keepdims=True)
+    owns = [
+        jnp.where(block == first, 1.0, 0.0),
+        jnp.where((block == last) & (last > first), 1.0, 0.0),
+    ]
     own_all = jnp.concatenate(owns, axis=0).astype(BF16)
     here = iota((blocks, GAUSS), 1) // ROWS == iota((blocks, GAUSS), 0)
     number = jnp.where(here, order + 1, 0)
     parts = jnp.concatenate(
-        [(number // 16).astype(F32), (number % 16).astype(F32)], axis=0
+        [(number >> 4).astype(F32), (number & 15).astype(F32)], axis=0
     ).astype(BF16)
     pick = jnp.where(iota((GAUSS, PIX), 0) % ROWS == iota((GAUSS, PIX), 1), 1.0, 0.0).astype(BF16)
     table = mm(parts, pick).astype(BF16)
@@ -422,12 +425,13 @@
 
 def step_first(message, right, damp, proj, select, start):
     wide = turned_pair(message)
-    product = product_of(message, wide) + damp * right
+    back = product_of(message, wide)
+    product = back + damp * right
     near = right - first_guess(start) * product
     out = to_message([project(proj[:, : PIX // 2], near)], select)
     sums = [
         jnp.zeros((1, 1), F32),
-        total(right * product),
+        total(right * back),
         total(near * near),
         total(near * right),
         total(near * product),
@@ -444,22 +448,23 @@
     product = product_of(message, wide[...])
     energy = jnp.sum(message[:, GAUSS // PIX * FEAT], axis=0, keepdims=True)[:, 0:1]
     start = start_ref[...]
-    guess, square = first_guess(start), start[:, 2:3]
+    guess, square, damped = first_guess(start), start[:, 2:3], start[:, 3:4]
     sums = message[0, GAUSS // PIX * FEAT :]
-    cross, nn, nb, ny, ndn = [sums[:, i : i + 1] for i in range(1, 6)]
-    step = square / cross
-    share = step / guess
-    rest = 1.0 - share
+    seen, nn, nb, ny, ndn = [sums[:, i : i + 1] for i in range(1, 6)]
+    cross = seen + damped
+    step, share, rest = square / cross, damped / cross, seen / cross
     square_now = share * share * nn + 2.0 * share * rest * nb + rest * rest * square
-    part = rest + square_now / square
+    ratio = square_now / square
+    part = rest + ratio
     bent = share * share * (energy + ndn) + 2.0 * share * part * ny + part * part * cross
     step_now = square_now / bent
     right, before = right_ref[...], product_ref[...]
     near = right - guess * before
-    solution[...] = step * right + step_now * (share * near + part * right)
+    residual = share * near + rest * right
+    solution[...] = step * right + step_now * (residual + ratio * right)
     first = pltpu.make_async_copy(solution, solution_hbm, sems.at[0])
     first.start()
-    final[...] = (right - step * before) - step_now * (
+    final[...] = residual - step_now * (
         share * (product + damp_ref[...] * near) + part * before
     )
     second = pltpu.make_async_copy(final, final_hbm, sems.at[1])

time: 113 us -> 113 us (level)
  no operation moved by 1% of the time
where the time goes in v8:
time: 113 us; the launch traced here: 112 us
  blocking collectives  102 us (90%)
  Pallas kernels  9.12 us (8%)
    all_to_all x4, blocking collectives, over_tiles(): lax.all_to_all(message, 'tiles', split_axis=0, concat_axis=0, tiled=True)  68.8 us
    all_to_all x2, blocking collectives, over_views(): lax.all_to_all(part, 'views', split_axis=0, concat_axis=0, tiled=True)  33.7 us
    pallas_call x5, Pallas kernels, call(): pl.pallas_call(kernel, out_shape=[jax.ShapeDtypeStruct(shape, dtype) for...  5.9 us

profile of v8, /device:TPU:1, one launch (start us, length us, event | category | flops | bytes accessed | tf_op | source)
XLA Modules:
  0.0 112.3 jit_solution(13138009470093219632)
XLA Ops:
  0.6 2.0 %begin.1 = (f32[64,1,640]{2,1,0:T(1,128)S(1)}, bf16[1024,512]{1,0:T(8,128)(2,1)S(1)}, f32[24,128]{1,0:T(8,128)S(1)}, f32[16,128]{1,0:T(8,128)S(1)}) custom-call(f32[59,512]{1,0:T(8,128)} %point_hbm.1, f32[59,512]{1,0:T(8,128)} %right_ref.1, f32[59,512]{1,0:T(8,128)} %damp_ref.1, f32[16,59]{1,0:T(8,128)} %bitcast.7, f32[12,1,128]{2,1,0:T(1,128)} %bitcast.8, ...), custom_call_target="tpu_custom_call" | custom-call | tf_op jit(solution)/shard_map/begin/pallas_call | solution.py:155
  2.7 25.2 %all_to_all.30.refs_0_ = f32[64,1,640]{2,1,0:T(1,128)S(1)} all-to-all(f32[64,1,640]{2,1,0:T(1,128)S(1)} %get-tuple-element.19), channel_id=1, replica_groups=mesh['views'=8,'tiles'=64] {'tiles'}, dimensions={0} | all-to-all | bytes 327680 | tf_op jit(solution)/shard_map/all_to_all | solution.py:528
  27.9 2.3 %render_first.1 = (f32[64,1,256]{2,1,0:T(1,128)S(1)}, f32[1024,128]{1,0:T(8,128)S(1)}, f32[1024,128]{1,0:T(8,128)S(1)}, f32[1024,128]{1,0:T(8,128)S(1)}, f32[16,...) custom-call(f32[64,1,640]{2,1,0:T(1,128)S(1)} %all_to_all.30.refs_0_, ...), custom_call_target="tpu_custom_call" | custom-call | tf_op jit(solution)/shard_map/render_first/pallas_call | solution.py:500
  30.2 14.9 %all_to_all.31.refs_0_ = f32[64,1,256]{2,1,0:T(1,128)S(1)} all-to-all(f32[64,1,256]{2,1,0:T(1,128)S(1)} %get-tuple-element.21), channel_id=1, replica_groups=mesh['views'=8,'tiles'=64] {'tiles'}, dimensions={0} | all-to-all | bytes 131072 | tf_op jit(solution)/shard_map/all_to_all | solution.py:528
  45.2 0.4 collect.1
  45.6 0.0 copy-start
  45.6 0.0 copy-start.1
  45.6 18.9 %all_to_all.32.refs_0_ = f32[8,72,128]{2,1,0:T(8,128)S(1)} all-to-all(f32[8,72,128]{2,1,0:T(8,128)S(1)} %collect.1), channel_id=1, replica_groups=mesh['views'=8,'tiles'=64] {'views'}, dimensions={0} | all-to-all | bytes 589824 | tf_op jit(solution)/shard_map/all_to_all | solution.py:531
  64.5 0.0 copy-done
  64.5 0.0 copy-done.1
  64.5 1.0 step_first.1
  65.6 14.6 %all_to_all.33.refs_0_ = f32[64,1,256]{2,1,0:T(1,128)S(1)} all-to-all(f32[64,1,256]{2,1,0:T(1,128)S(1)} %get-tuple-element.25), channel_id=1, replica_groups=mesh['views'=8,'tiles'=64] {'tiles'}, dimensions={0} | all-to-all | bytes 131072 | tf_op jit(solution)/shard_map/all_to_all | solution.py:528
  80.1 1.6 %render_again.1 = f32[64,1,384]{2,1,0:T(1,128)S(1)} custom-call(f32[64,1,256]{2,1,0:T(1,128)S(1)} %all_to_all.33.refs_0_, f32[1,128]{1,0:T(1,128)S(1)} %get-tuple-element.26.refs_1_, f32[24,128]{1,0:T(8,128)S(1)} %get-tuple-element.20.refs_1_.refs_2_, f32[1024,128]{1,0:T(8,128)S(1)} %get-tuple-element.27.refs_3_, f32[1024,128]{1,0:T(8,128)S(1)} %get-tuple-element.28.refs_4_, ...), custom_call_target="tpu_custom_call" | custom-call | tf_op jit(solution)/shard_map/render_again/pallas_call | solution.py:500
  81.7 14.0 %all_to_all.34.refs_0_ = f32[64,1,384]{2,1,0:T(1,128)S(1)} all-to-all(f32[64,1,384]{2,1,0:T(1,128)S(1)} %render_again.1), channel_id=1, replica_groups=mesh['views'=8,'tiles'=64] {'tiles'}, dimensions={0} | all-to-all | bytes 196608 | tf_op jit(solution)/shard_map/all_to_all | solution.py:528
  95.8 0.5 collect_last.1
  96.3 14.8 %all_to_all.35.message_ref = f32[8,65,1,128]{3,2,1,0:T(1,128)S(1)} all-to-all(f32[8,65,1,128]{3,2,1,0:T(1,128)S(1)} %collect_last.1), channel_id=1, replica_groups=mesh['views'=8,'tiles'=64] {'views'}, dimensions={0} | all-to-all | bytes 532480 | tf_op jit(solution)/shard_map/all_to_all | solution.py:531
  111.1 1.2 %finish.1 = (f32[59,512]{1,0:T(8,128)}, f32[59,512]{1,0:T(8,128)}) custom-call(f32[8,65,1,128]{3,2,1,0:T(1,128)S(1)} %all_to_all.35.message_ref, f32[59,512]{1,0:T(8,128)S(1)} %copy-done, f32[59,512]{1,0:T(8,128)S(1)} %copy-done.1, f32[59,512]{1,0:T(8,128)S(1)} %get-tuple-element.34.product_ref, bf16[128,256]{1,0:T(8,128)(2,1)S(1)} %get-tuple-element.35.wide, ...), custom_call_target="tpu_custom_call" | custom-call | tf_op jit(solution)/shard_map/finish/pallas_call | solution.py:478
Async XLA Ops:
  45.6 18.9 %copy-start = (f32[59,512]{1,0:T(8,128)S(1)}, f32[59,512]{1,0:T(8,128)}, u32[]{:S(2)}) copy-start(f32[59,512]{1,0:T(8,128)} %right_ref.1) | copy-start | bytes 362500
  45.6 18.9 %copy-start.1 = (f32[59,512]{1,0:T(8,128)S(1)}, f32[59,512]{1,0:T(8,128)}, u32[]{:S(2)}) copy-start(f32[59,512]{1,0:T(8,128)} %damp_ref.1) | copy-start | bytes 362500

commit v9 on v8

--- a/solution.py
+++ b/solution.py
@@ -437,18 +437,18 @@
         total(near * product),
         total(damp * near * near),
     ]
-    return out, product, wide, lanes(sums, 1)
+    return out, product, near, wide, lanes(sums, 1)
 
 
 def finish_kernel(
-    message_ref, right_ref, damp_ref, product_ref, wide, start_ref,
+    message_ref, right_ref, damp_ref, product_ref, near_ref, wide, start_ref,
     solution_hbm, final_hbm, solution, final, sems,
 ):
     message = message_ref[:, :, 0, :]
     product = product_of(message, wide[...])
     energy = jnp.sum(message[:, GAUSS // PIX * FEAT], axis=0, keepdims=True)[:, 0:1]
     start = start_ref[...]
-    guess, square, damped = first_guess(start), start[:, 2:3], start[:, 3:4]
+    square, damped = start[:, 2:3], start[:, 3:4]
     sums = message[0, GAUSS // PIX * FEAT :]
     seen, nn, nb, ny, ndn = [sums[:, i : i + 1] for i in range(1, 6)]
     cross = seen + damped
@@ -458,8 +458,7 @@
     part = rest + ratio
     bent = share * share * (energy + ndn) + 2.0 * share * part * ny + part * part * cross
     step_now = square_now / bent
-    right, before = right_ref[...], product_ref[...]
-    near = right - guess * before
+    right, before, near = right_ref[...], product_ref[...], near_ref[...]
     residual = share * near + rest * right
     solution[...] = step * right + step_now * (residual + ratio * right)
     first = pltpu.make_async_copy(solution, solution_hbm, sems.at[0])
@@ -548,10 +547,11 @@
     gather = functools.partial(collect, views)
     gather.__name__ = "collect"
     (part,) = call(gather, [part_shape], over_tiles(message), select, proj)
-    message, product, wide, sums = call(
+    message, product, near, wide, sums = call(
         step_first,
         [
             ((OWNERS, 1, width), F32),
+            ((PARAMS, GAUSS), F32),
             ((PARAMS, GAUSS), F32),
             ((PIX, 2 * views * FEAT), BF16),
             ((1, PIX), F32),
@@ -568,7 +568,7 @@
     last_shape = ((views, GAUSS // PIX * FEAT + 1, 1, PIX), F32)
     (part,) = call(gather, [last_shape], over_tiles(message), select)
     return tuple(
-        finish(over_views(part), right_side, damping, product, wide, start)
+        finish(over_views(part), right_side, damping, product, near, wide, start)
     )
 
 

time: 113 us -> 113 us (level)
  no operation moved by 1% of the time
where the time goes in v9:
time: 113 us; the launch traced here: 112 us
  blocking collectives  102 us (90%)
  Pallas kernels  9.07 us (8%)
    all_to_all x4, blocking collectives, over_tiles(): lax.all_to_all(message, 'tiles', split_axis=0, concat_axis=0, tiled=True)  68.8 us
    all_to_all x2, blocking collectives, over_views(): lax.all_to_all(part, 'views', split_axis=0, concat_axis=0, tiled=True)  33.7 us
    pallas_call x5, Pallas kernels, call(): pl.pallas_call(kernel, out_shape=[jax.ShapeDtypeStruct(shape, dtype) for...  5.9 us

profile of v9, /device:TPU:1, one launch (start us, length us, event | category | flops | bytes accessed | tf_op | source)
XLA Modules:
  0.0 112.2 jit_solution(10294573419400030623)
XLA Ops:
  0.6 2.0 %begin.1 = (f32[64,1,640]{2,1,0:T(1,128)S(1)}, bf16[1024,512]{1,0:T(8,128)(2,1)S(1)}, f32[24,128]{1,0:T(8,128)S(1)}, f32[16,128]{1,0:T(8,128)S(1)}) custom-call(f32[59,512]{1,0:T(8,128)} %point_hbm.1, f32[59,512]{1,0:T(8,128)} %right_ref.1, f32[59,512]{1,0:T(8,128)} %damp_ref.1, f32[16,59]{1,0:T(8,128)} %bitcast.7, f32[12,1,128]{2,1,0:T(1,128)} %bitcast.8, ...), custom_call_target="tpu_custom_call" | custom-call | tf_op jit(solution)/shard_map/begin/pallas_call | solution.py:155
  2.7 25.2 %all_to_all.30.refs_0_ = f32[64,1,640]{2,1,0:T(1,128)S(1)} all-to-all(f32[64,1,640]{2,1,0:T(1,128)S(1)} %get-tuple-element.20), channel_id=1, replica_groups=mesh['views'=8,'tiles'=64] {'tiles'}, dimensions={0} | all-to-all | bytes 327680 | tf_op jit(solution)/shard_map/all_to_all | solution.py:527
  27.9 2.3 %render_first.1 = (f32[64,1,256]{2,1,0:T(1,128)S(1)}, f32[1024,128]{1,0:T(8,128)S(1)}, f32[1024,128]{1,0:T(8,128)S(1)}, f32[1024,128]{1,0:T(8,128)S(1)}, f32[16,...) custom-call(f32[64,1,640]{2,1,0:T(1,128)S(1)} %all_to_all.30.refs_0_, ...), custom_call_target="tpu_custom_call" | custom-call | tf_op jit(solution)/shard_map/render_first/pallas_call | solution.py:499
  30.2 14.9 %all_to_all.31.refs_0_ = f32[64,1,256]{2,1,0:T(1,128)S(1)} all-to-all(f32[64,1,256]{2,1,0:T(1,128)S(1)} %get-tuple-element.22), channel_id=1, replica_groups=mesh['views'=8,'tiles'=64] {'tiles'}, dimensions={0} | all-to-all | bytes 131072 | tf_op jit(solution)/shard_map/all_to_all | solution.py:527
  45.2 0.4 collect.1
  45.6 0.0 copy-start
  45.6 0.0 copy-start.1
  45.6 18.9 %all_to_all.32.refs_0_ = f32[8,72,128]{2,1,0:T(8,128)S(1)} all-to-all(f32[8,72,128]{2,1,0:T(8,128)S(1)} %collect.1), channel_id=1, replica_groups=mesh['views'=8,'tiles'=64] {'views'}, dimensions={0} | all-to-all | bytes 589824 | tf_op jit(solution)/shard_map/all_to_all | solution.py:530
  64.5 0.0 copy-done
  64.5 0.0 copy-done.1
  64.5 1.0 step_first.1
  65.6 14.6 %all_to_all.33.refs_0_ = f32[64,1,256]{2,1,0:T(1,128)S(1)} all-to-all(f32[64,1,256]{2,1,0:T(1,128)S(1)} %get-tuple-element.26), channel_id=1, replica_groups=mesh['views'=8,'tiles'=64] {'tiles'}, dimensions={0} | all-to-all | bytes 131072 | tf_op jit(solution)/shard_map/all_to_all | solution.py:527
  80.1 1.6 %render_again.1 = f32[64,1,384]{2,1,0:T(1,128)S(1)} custom-call(f32[64,1,256]{2,1,0:T(1,128)S(1)} %all_to_all.33.refs_0_, f32[1,128]{1,0:T(1,128)S(1)} %get-tuple-element.27.refs_1_, f32[24,128]{1,0:T(8,128)S(1)} %get-tuple-element.21.refs_1_.refs_2_, f32[1024,128]{1,0:T(8,128)S(1)} %get-tuple-element.28.refs_3_, f32[1024,128]{1,0:T(8,128)S(1)} %get-tuple-element.29.refs_4_, ...), custom_call_target="tpu_custom_call" | custom-call | tf_op jit(solution)/shard_map/render_again/pallas_call | solution.py:499
  81.7 14.0 %all_to_all.34.refs_0_ = f32[64,1,384]{2,1,0:T(1,128)S(1)} all-to-all(f32[64,1,384]{2,1,0:T(1,128)S(1)} %render_again.1), channel_id=1, replica_groups=mesh['views'=8,'tiles'=64] {'tiles'}, dimensions={0} | all-to-all | bytes 196608 | tf_op jit(solution)/shard_map/all_to_all | solution.py:527
  95.8 0.5 collect_last.1
  96.3 14.8 %all_to_all.35.message_ref = f32[8,65,1,128]{3,2,1,0:T(1,128)S(1)} all-to-all(f32[8,65,1,128]{3,2,1,0:T(1,128)S(1)} %collect_last.1), channel_id=1, replica_groups=mesh['views'=8,'tiles'=64] {'views'}, dimensions={0} | all-to-all | bytes 532480 | tf_op jit(solution)/shard_map/all_to_all | solution.py:530
  111.1 1.1 %finish.1 = (f32[59,512]{1,0:T(8,128)}, f32[59,512]{1,0:T(8,128)}) custom-call(f32[8,65,1,128]{3,2,1,0:T(1,128)S(1)} %all_to_all.35.message_ref, f32[59,512]{1,0:T(8,128)S(1)} %copy-done, f32[59,512]{1,0:T(8,128)S(1)} %copy-done.1, f32[59,512]{1,0:T(8,128)S(1)} %get-tuple-element.35.product_ref, f32[59,512]{1,0:T(8,128)S(1)} %get-tuple-element.36.near_ref, ...), custom_call_target="tpu_custom_call" | custom-call | tf_op jit(solution)/shard_map/finish/pallas_call | solution.py:477
Async XLA Ops:
  45.6 18.9 %copy-start = (f32[59,512]{1,0:T(8,128)S(1)}, f32[59,512]{1,0:T(8,128)}, u32[]{:S(2)}) copy-start(f32[59,512]{1,0:T(8,128)} %right_ref.1) | copy-start | bytes 362500
  45.6 18.9 %copy-start.1 = (f32[59,512]{1,0:T(8,128)S(1)}, f32[59,512]{1,0:T(8,128)}, u32[]{:S(2)}) copy-start(f32[59,512]{1,0:T(8,128)} %damp_ref.1) | copy-start | bytes 362500

commit v10 on v9

--- a/solution.py
+++ b/solution.py
@@ -376,11 +376,10 @@
     return jnp.broadcast_to(part[None], (views,) + part.shape)
 
 
-def collect_last(views, message, select):
+def collect_last(message, select):
     parts = gathered_parts(message, select)
     tail = jnp.sum(message[:, PIECES * FEAT :], axis=0, keepdims=True)
-    part = jnp.concatenate(parts + [tail], axis=0)
-    return jnp.broadcast_to(part[None], (views,) + part.shape)
+    return jnp.concatenate(parts + [tail], axis=0)
 
 
 def turned_pair(message):
@@ -563,10 +562,9 @@
         [((OWNERS, 1, width + PIX), F32)],
         over_tiles(message), sums, aux, alphas, clears, weights, prim, blended, front, behind,
     )
-    gather = functools.partial(collect_last, views)
-    gather.__name__ = "collect_last"
-    last_shape = ((views, GAUSS // PIX * FEAT + 1, 1, PIX), F32)
-    (part,) = call(gather, [last_shape], over_tiles(message), select)
+    last_shape = ((GAUSS // PIX * FEAT + 1, PIX), F32)
+    (part,) = call(collect_last, [last_shape], over_tiles(message), select)
+    part = jnp.broadcast_to(part[None, :, None], (views, part.shape[0], 1, PIX))
     return tuple(
         finish(over_views(part), right_side, damping, product, near, wide, start)
     )

time: 113 us -> 113 us (level)
  no operation moved by 1% of the time
where the time goes in v10:
time: 113 us; the launch traced here: 112 us
  blocking collectives  102 us (90%)
  Pallas kernels  8.92 us (8%)
    all_to_all x4, blocking collectives, over_tiles(): lax.all_to_all(message, 'tiles', split_axis=0, concat_axis=0, tiled=True)  68.8 us
    all_to_all x2, blocking collectives, over_views(): lax.all_to_all(part, 'views', split_axis=0, concat_axis=0, tiled=True)  33.7 us
    pallas_call x5, Pallas kernels, call(): pl.pallas_call(kernel, out_shape=[jax.ShapeDtypeStruct(shape, dtype) for...  5.75 us

profile of v10, /device:TPU:1, one launch (start us, length us, event | category | flops | bytes accessed | tf_op | source)
XLA Modules:
  0.0 112.2 jit_solution(8326651070176233728)
XLA Ops:
  0.6 2.0 %begin.1 = (f32[64,1,640]{2,1,0:T(1,128)S(1)}, bf16[1024,512]{1,0:T(8,128)(2,1)S(1)}, f32[24,128]{1,0:T(8,128)S(1)}, f32[16,128]{1,0:T(8,128)S(1)}) custom-call(f32[59,512]{1,0:T(8,128)} %point_hbm.1, f32[59,512]{1,0:T(8,128)} %right_ref.1, f32[59,512]{1,0:T(8,128)} %damp_ref.1, f32[16,59]{1,0:T(8,128)} %bitcast.7, f32[12,1,128]{2,1,0:T(1,128)} %bitcast.8, ...), custom_call_target="tpu_custom_call" | custom-call | tf_op jit(solution)/shard_map/begin/pallas_call | solution.py:155
  2.7 25.2 %all_to_all.30.refs_0_ = f32[64,1,640]{2,1,0:T(1,128)S(1)} all-to-all(f32[64,1,640]{2,1,0:T(1,128)S(1)} %get-tuple-element.20), channel_id=1, replica_groups=mesh['views'=8,'tiles'=64] {'tiles'}, dimensions={0} | all-to-all | bytes 327680 | tf_op jit(solution)/shard_map/all_to_all | solution.py:526
  27.9 2.3 %render_first.1 = (f32[64,1,256]{2,1,0:T(1,128)S(1)}, f32[1024,128]{1,0:T(8,128)S(1)}, f32[1024,128]{1,0:T(8,128)S(1)}, f32[1024,128]{1,0:T(8,128)S(1)}, f32[16,...) custom-call(f32[64,1,640]{2,1,0:T(1,128)S(1)} %all_to_all.30.refs_0_, ...), custom_call_target="tpu_custom_call" | custom-call | tf_op jit(solution)/shard_map/render_first/pallas_call | solution.py:498
  30.2 14.9 %all_to_all.31.refs_0_ = f32[64,1,256]{2,1,0:T(1,128)S(1)} all-to-all(f32[64,1,256]{2,1,0:T(1,128)S(1)} %get-tuple-element.22), channel_id=1, replica_groups=mesh['views'=8,'tiles'=64] {'tiles'}, dimensions={0} | all-to-all | bytes 131072 | tf_op jit(solution)/shard_map/all_to_all | solution.py:526
  45.2 0.4 collect.1
  45.6 0.0 copy-start
  45.6 0.0 copy-start.1
  45.6 18.9 %all_to_all.32.refs_0_ = f32[8,72,128]{2,1,0:T(8,128)S(1)} all-to-all(f32[8,72,128]{2,1,0:T(8,128)S(1)} %collect.1), channel_id=1, replica_groups=mesh['views'=8,'tiles'=64] {'views'}, dimensions={0} | all-to-all | bytes 589824 | tf_op jit(solution)/shard_map/all_to_all | solution.py:529
  64.5 0.0 copy-done
  64.5 0.0 copy-done.1
  64.5 1.0 step_first.1
  65.6 14.6 %all_to_all.33.refs_0_ = f32[64,1,256]{2,1,0:T(1,128)S(1)} all-to-all(f32[64,1,256]{2,1,0:T(1,128)S(1)} %get-tuple-element.26), channel_id=1, replica_groups=mesh['views'=8,'tiles'=64] {'tiles'}, dimensions={0} | all-to-all | bytes 131072 | tf_op jit(solution)/shard_map/all_to_all | solution.py:526
  80.1 1.6 %render_again.1 = f32[64,1,384]{2,1,0:T(1,128)S(1)} custom-call(f32[64,1,256]{2,1,0:T(1,128)S(1)} %all_to_all.33.refs_0_, f32[1,128]{1,0:T(1,128)S(1)} %get-tuple-element.27.refs_1_, f32[24,128]{1,0:T(8,128)S(1)} %get-tuple-element.21.refs_1_.refs_2_, f32[1024,128]{1,0:T(8,128)S(1)} %get-tuple-element.28.refs_3_, f32[1024,128]{1,0:T(8,128)S(1)} %get-tuple-element.29.refs_4_, ...), custom_call_target="tpu_custom_call" | custom-call | tf_op jit(solution)/shard_map/render_again/pallas_call | solution.py:498
  81.7 14.0 %all_to_all.34.refs_0_ = f32[64,1,384]{2,1,0:T(1,128)S(1)} all-to-all(f32[64,1,384]{2,1,0:T(1,128)S(1)} %render_again.1), channel_id=1, replica_groups=mesh['views'=8,'tiles'=64] {'tiles'}, dimensions={0} | all-to-all | bytes 196608 | tf_op jit(solution)/shard_map/all_to_all | solution.py:526
  95.8 0.4 collect_last.1
  96.2 0.2 broadcast_in_dim.2
  96.3 14.8 %all_to_all.35.message_ref = f32[8,65,1,128]{3,2,1,0:T(1,128)S(1)} all-to-all(f32[8,65,1,128]{3,2,1,0:T(1,128)S(1)} %broadcast_in_dim.2), channel_id=1, replica_groups=mesh['views'=8,'tiles'=64] {'views'}, dimensions={0} | all-to-all | bytes 532480 | tf_op jit(solution)/shard_map/all_to_all | solution.py:529
  111.1 1.1 %finish.1 = (f32[59,512]{1,0:T(8,128)}, f32[59,512]{1,0:T(8,128)}) custom-call(f32[8,65,1,128]{3,2,1,0:T(1,128)S(1)} %all_to_all.35.message_ref, f32[59,512]{1,0:T(8,128)S(1)} %copy-done, f32[59,512]{1,0:T(8,128)S(1)} %copy-done.1, f32[59,512]{1,0:T(8,128)S(1)} %get-tuple-element.35.product_ref, f32[59,512]{1,0:T(8,128)S(1)} %get-tuple-element.36.near_ref, ...), custom_call_target="tpu_custom_call" | custom-call | tf_op jit(solution)/shard_map/finish/pallas_call | solution.py:476
Async XLA Ops:
  45.6 18.9 %copy-start = (f32[59,512]{1,0:T(8,128)S(1)}, f32[59,512]{1,0:T(8,128)}, u32[]{:S(2)}) copy-start(f32[59,512]{1,0:T(8,128)} %right_ref.1) | copy-start | bytes 362500
  45.6 18.9 %copy-start.1 = (f32[59,512]{1,0:T(8,128)S(1)}, f32[59,512]{1,0:T(8,128)}, u32[]{:S(2)}) copy-start(f32[59,512]{1,0:T(8,128)} %damp_ref.1) | copy-start | bytes 362500
